TPU v7x, 32 devices: a whole 2x2x4 slice. The times are simulated.
32 devices in a mesh: rows: 16 (over z, y, core), cols: 2 (over x).
Axes of the slice: x: 2, y: 2, z: 4, core: 2. Of those that a mesh axis runs over, the one named last changes fastest.
Arguments:
- residual: bfloat16 [2, 8192, 8192], P(None, 'rows', 'cols'), may hold values from -6 to 6
- field_slopes: bfloat16 [4, 8192, 8192], P(None, 'rows', 'cols'), may hold values from -6 to 6
- source_tile: int32 [2, 8192, 64], P(None, 'rows', 'cols'), may hold values from 0 to 31
- row_shift: int32 [2, 8192, 64], P(None, 'rows', 'cols'), may hold values from -8 to 8
- pixel_shift: int32 [2, 8192, 64], P(None, 'rows', 'cols'), may hold values from -2 to 2
- fraction: float32 [2, 8192, 64], P(None, 'rows', 'cols'), may hold values from 0 to 1
Outputs:
- potential_step: float32 [8192, 8192], P('rows', 'cols')
Inputs may be any that keep to these rules, and one draw needn't show every extreme that they name: `source_tile`: a tile number inside the group of 32 tiles that holds the destination tile.
All inputs are finite; a program needn't handle non-finite values.
Results may differ from a plain program's by a relative error of at most 0.0003.
Values may be sent and summed in bfloat16 or wider, within the bound.
No kernel may reach another device: no remote copies, remote signals or barrier semaphores. Data moves between devices by JAX's collectives and lax.ppermute only.
A program may use at most 256 MiB of HBM per device.

v0:
```python
import math

import jax
import jax.numpy as jnp
from jax import lax
from jax.sharding import PartitionSpec as P

N = 8192
TILE = 128
PAIRS = 2
HALO = 8
SHIFT = 2


local_weight = 0.5
highest = lax.Precision.HIGHEST


def with_halo(x, sides, width):
    for axis, dim in sides:
        peers, length = (lax.axis_size(axis), x.shape[dim])
        up = [(i, (i + 1) % peers) for i in range(peers - 1)]
        down = [(j, i) for i, j in up]
        last = lax.slice_in_dim(x, length - width, length, axis=dim)
        first = lax.slice_in_dim(x, 0, width, axis=dim)
        before = lax.ppermute(last, axis, up)
        after = lax.ppermute(first, axis, down)
        x = jnp.concatenate([before, x, after], axis=dim)
    return x


def phase_pair(phases, length, direction):
    angles = phases.astype(jnp.float32) * (direction * 2.0 * math.pi / length)
    return (jnp.cos(angles), jnp.sin(angles))


def fourier_matrix(length, direction):
    counter = jnp.arange(length, dtype=jnp.int32)
    cosine, sine_part = phase_pair(counter[:, None] * counter[None, :] % length, length, direction)
    return jnp.stack([jnp.stack([cosine, sine_part], 1), jnp.stack([-sine_part, cosine], 1)], 0)


def rotate(values, cosine, sine_part):
    real_part = values[0] * cosine - values[1] * sine_part
    imag_part = values[0] * sine_part + values[1] * cosine
    return jnp.stack([real_part, imag_part])


def contract_indices(formula, values, matrix):
    return jnp.einsum(
        formula, values, matrix, precision=highest, preferred_element_type=jnp.float32
    )


def signed_wave(counter):
    middle = N // 2
    shifted = jnp.where(counter > middle, counter - N, counter)
    shifted = jnp.where(counter == middle, 0, shifted)
    return shifted.astype(jnp.float32) * (2.0 * math.pi / N)


def across_columns(values):
    return lax.all_to_all(values, "cols", split_axis=1, concat_axis=2, tiled=True)


def across_rows(values):
    return lax.all_to_all(values, "rows", split_axis=3, concat_axis=1, tiled=True)


def remap_tiles(padded, source_tile, row_shift, pixel_shift, fraction):
    rows_dev = padded.shape[1] - 2 * HALO
    tiles_dev = padded.shape[2] // TILE
    tile_rows = padded.reshape(2, (rows_dev + 2 * HALO) * tiles_dev, TILE)
    row_index = jnp.arange(rows_dev, dtype=jnp.int32)[None, :, None]
    flat_index = (row_index + HALO + row_shift) * tiles_dev + source_tile
    picked = jnp.take(tile_rows, flat_index.reshape(-1), axis=1)
    picked = picked.reshape(2, PAIRS, rows_dev, tiles_dev, TILE)
    widened = jnp.pad(picked, ((0, 0), (0, 0), (0, 0), (0, 0), (SHIFT + 1, SHIFT + 1)))
    pulled = jnp.zeros((2, rows_dev, tiles_dev, TILE), jnp.float32)
    for offset in range(-SHIFT, SHIFT + 2):
        weights = jnp.where(pixel_shift == offset, 1.0 - fraction, 0.0)
        weights = weights + jnp.where(pixel_shift + 1 == offset, fraction, 0.0)
        start_at = SHIFT + 1 + offset
        window = widened[..., start_at : start_at + TILE].astype(jnp.float32)
        pulled = pulled + jnp.sum(window * weights[None, :, :, :, None], axis=1)
    return pulled.reshape(2, rows_dev, tiles_dev * TILE)


def weigh_spectra(power_spectra, row_wave, col_wave):
    floored_wavenumber = 8.0 * math.pi / N
    weight = local_weight + 1.0 / (
        row_wave * row_wave + col_wave * col_wave + floored_wavenumber * floored_wavenumber
    )
    real_part = weight * (col_wave * power_spectra[1, 0] - row_wave * power_spectra[0, 0])
    imag_part = -weight * (col_wave * power_spectra[0, 0] + row_wave * power_spectra[1, 0])
    return jnp.stack([real_part, imag_part])


def per_device(residual, field_slopes, source_tile, row_shift, pixel_shift, fraction):
    padded = with_halo(residual, (("rows", 1),), HALO)
    pulled = remap_tiles(padded, source_tile, row_shift, pixel_shift, fraction)
    slopes = field_slopes.astype(jnp.float32)
    flow_across = -(pulled[0] * slopes[0] + pulled[1] * slopes[1])
    downward_flow = -(pulled[0] * slopes[2] + pulled[1] * slopes[3])
    rows_dev = residual.shape[1]
    cols_dev = residual.shape[2]
    rows_count = lax.axis_size("rows")
    cols_count = lax.axis_size("cols")
    part_rows = rows_dev // cols_count
    spread = rows_count // cols_count
    col_index = lax.axis_index("cols")
    row_place = lax.axis_index("rows")
    compact_forward_transform = fourier_matrix(rows_count, -1)
    large_forward = fourier_matrix(rows_dev, -1)
    compact_inverse_transform = fourier_matrix(rows_count, 1)
    large_inverse = fourier_matrix(rows_dev, 1)
    wave_index = jnp.arange(rows_count, dtype=jnp.int32)
    pixel_index = jnp.arange(rows_dev, dtype=jnp.int32)
    band = col_index * part_rows + jnp.arange(part_rows, dtype=jnp.int32)
    stacked_planes = jnp.stack([flow_across, downward_flow]).reshape(2, rows_dev, 1, cols_dev)
    stacked_planes = across_columns(stacked_planes).reshape(2, part_rows, rows_count, rows_dev)
    power_spectra = contract_indices("pibc,pbqk->qikc", stacked_planes, compact_forward_transform)[
        :, None
    ]
    cosine, sine_part = phase_pair(wave_index[:, None] * pixel_index[None, :], N, -1)
    power_spectra = rotate(power_spectra, cosine, sine_part)
    power_spectra = contract_indices("pfikc,pcql->qfikl", power_spectra, large_forward)
    fields = power_spectra.shape[1]
    back_cos, back_sin = phase_pair(wave_index[:, None] * pixel_index[None, :], N, 1)
    power_spectra = across_rows(power_spectra)
    power_spectra = power_spectra.reshape(2, fields, rows_count, part_rows, rows_dev)
    power_spectra = contract_indices("pfrik,prqm->qfmik", power_spectra, compact_forward_transform)
    band_cos, band_sin = phase_pair(wave_index[:, None] * band[None, :], N, -1)
    power_spectra = rotate(power_spectra, band_cos[:, :, None], band_sin[:, :, None])
    power_spectra = across_columns(
        power_spectra.reshape(2 * fields, rows_count, part_rows, rows_dev)
    )
    power_spectra = power_spectra.reshape(2, fields, spread, rows_dev, rows_dev)
    power_spectra = contract_indices("pfmsk,psql->qfmlk", power_spectra, large_forward)
    row_freq = (
        rows_count * pixel_index[None, :]
        + (col_index * spread + jnp.arange(spread, dtype=jnp.int32))[:, None]
    )
    row_wave = signed_wave(row_freq)[:, :, None]
    col_wave = signed_wave(rows_count * pixel_index + row_place)
    mixed = weigh_spectra(power_spectra, row_wave, col_wave)
    mixed = contract_indices("pmlk,plqs->qsmk", mixed, large_inverse)
    mixed = across_columns(mixed)
    band_cos, band_sin = phase_pair(band[:, None] * wave_index[None, :], N, 1)
    mixed = rotate(mixed, band_cos[:, :, None], band_sin[:, :, None])
    mixed = contract_indices("pimk,pmqr->qirk", mixed, compact_inverse_transform)
    mixed = across_rows(mixed.reshape(2, 1, part_rows, rows_count, rows_dev))
    mixed = mixed.reshape(2, rows_count, part_rows, rows_dev)
    mixed = contract_indices("pnik,pkqa->qina", mixed, large_inverse)
    mixed = rotate(mixed, back_cos, back_sin)
    image = jnp.einsum(
        "pina,pnb->iba",
        mixed,
        compact_inverse_transform[:, :, 0, :],
        precision=highest,
        preferred_element_type=jnp.float32,
    )
    image = image.reshape(part_rows, cols_count, cols_dev) * (1.0 / (N * N))
    return lax.all_to_all(image, "cols", split_axis=1, concat_axis=0, tiled=True).reshape(
        rows_dev, cols_dev
    )


def solution(mesh):
    return jax.shard_map(
        per_device,
        mesh=mesh,
        in_specs=(
            P(None, "rows", "cols"),
            P(None, "rows", "cols"),
            P(None, "rows", "cols"),
            P(None, "rows", "cols"),
            P(None, "rows", "cols"),
            P(None, "rows", "cols"),
        ),
        out_specs=P("rows", "cols"),
        check_vma=False,
    )
```

profile of v0, /device:TPU:12, one launch (start us, length us, event | category | flops | bytes accessed | tf_op | source)
XLA Modules:
  0.0 3025.1 jit_solution(18041890378568504007)
XLA Ops:
  10.3 18.6 convert_element_type.195
  29.0 7.5 pad_maximum_fusion.2
  36.5 14.1 reshape.681
  50.6 60.3 %copy.115 = bf16[2,16896,128]{2,0,1:T(2,128)(2,1)} copy(bf16[2,16896,128]{2,1,0:T(8,128)(2,1)} %reshape.681) | data formatting | bytes 17301504 | tf_op jit(solution)/shard_map/reshape | solution.py:73
  111.0 216.5 %gather_fusion = bf16[32768,2,128]{2,1,0:T(2,128)(2,1)} fusion(bf16[2,16896,128]{2,0,1:T(2,128)(2,1)} %copy.115, s32[32768]{0:T(1024)S(1)} %broadcast_clamp_fusion), kind=kCustom, calls=%fused_computation | custom fusion | bytes 33685504 | tf_op jit(solution)/shard_map/jit(_take)/gather | solution.py:76
  327.5 115.1 %multiply_reduce_fusion.3 = (f32[2,512,32,128]{3,0,2,1:T(2,128)}, bf16[2,2,512,32,128]{4,0,3,2,1:T(2,128)(2,1)S(1)}) fusion(f32[2,512,32]{2,1,0:T(8,128)S(1)} %copy.118, bf16[2,2,512,32,128]{4,0,3,2,1:T(2,128)(2,1)} %bitcast.226, pred[2,512,32]{2,1,0:T(8,128)(4,1)S(1)} %copy.113), kind=kLoop, calls=%fused_computation.4 | loop fusion | flops 29360128 | bytes 50495488 | tf_op jit(solution)/shard_map/reduce_sum | solution.py:85
  442.5 86.0 %multiply_reduce_fusion = f32[2,512,32,128]{3,0,2,1:T(2,128)} fusion(f32[2,512,32]{2,1,0:T(8,128)S(1)} %copy.121, bf16[2,2,512,32,128]{4,0,3,2,1:T(2,128)(2,1)S(1)} %get-tuple-element.44), kind=kLoop, calls=%fused_computation.1 | loop fusion | flops 20971520 | bytes 33685504 | tf_op jit(solution)/shard_map/reduce_sum | solution.py:85
  528.6 85.9 %multiply_reduce_fusion.1 = f32[2,512,32,128]{3,0,2,1:T(2,128)} fusion(f32[2,512,32]{2,1,0:T(8,128)S(1)} %copy.120, bf16[2,2,512,32,128]{4,0,3,2,1:T(2,128)(2,1)S(1)} %get-tuple-element.44), kind=kLoop, calls=%fused_computation.2 | loop fusion | flops 20971520 | bytes 33685504 | tf_op jit(solution)/shard_map/reduce_sum | solution.py:85
  614.5 85.9 %multiply_reduce_fusion.2 = f32[2,512,32,128]{3,0,2,1:T(2,128)} fusion(f32[2,512,32]{2,1,0:T(8,128)S(1)} %copy.119, bf16[2,2,512,32,128]{4,0,3,2,1:T(2,128)(2,1)S(1)} %get-tuple-element.44), kind=kLoop, calls=%fused_computation.3 | loop fusion | flops 20971520 | bytes 33685504 | tf_op jit(solution)/shard_map/reduce_sum | solution.py:85
  700.4 85.9 %multiply_reduce_fusion.5 = f32[2,512,32,128]{3,0,2,1:T(2,128)} fusion(f32[2,512,32]{2,1,0:T(8,128)S(1)} %copy.116, bf16[2,2,512,32,128]{4,0,3,2,1:T(2,128)(2,1)S(1)} %get-tuple-element.44), kind=kLoop, calls=%fused_computation.6 | loop fusion | flops 20971520 | bytes 33685504 | tf_op jit(solution)/shard_map/reduce_sum | solution.py:85
  786.3 85.9 %multiply_reduce_fusion.4 = f32[2,512,32,128]{3,0,2,1:T(2,128)} fusion(f32[2,512,32]{2,1,0:T(8,128)S(1)} %copy.117, bf16[2,2,512,32,128]{4,0,3,2,1:T(2,128)(2,1)S(1)} %get-tuple-element.44), kind=kLoop, calls=%fused_computation.5 | loop fusion | flops 20971520 | bytes 33685504 | tf_op jit(solution)/shard_map/reduce_sum | solution.py:85
  872.2 40.2 %add_add_fusion = f32[8,512,8,128]{3,0,2,1:T(8,128)} fusion(f32[8,512,8,128]{3,0,2,1:T(8,128)} %bitcast.220, f32[8,512,8,128]{3,0,2,1:T(8,128)} %bitcast.221, f32[8,512,8,128]{3,0,2,1:T(8,128)} %bitcast.222, f32[8,512,8,128]{3,0,2,1:T(8,128)} %bitcast.219, f32[8,512,8,128]{3,0,2,1:T(8,128)} %bitcast.223, f32[8,512,8,128]{3,0,2,1:T(8,128)} %bitcast.224), kind=kLoop, calls=%fused_computation.29 | loop fusion | flops 20971520 | bytes 117440512 | tf_op jit(solution)/shard_map/add | solution.py:85
  912.4 56.0 %slice_reduce_fusion.1 = (f32[512,32,128]{2,1,0:T(8,128)}, f32[512,32,128]{2,1,0:T(8,128)}) fusion(f32[2,512,32,128]{3,0,2,1:T(2,128)} %bitcast.225), kind=kLoop, calls=%fused_computation.44 | loop fusion | bytes 33554432 | tf_op jit(solution)/shard_map/slice | solution.py:103
  968.4 9.4 squeeze.16
  977.8 9.4 squeeze.15
  987.2 24.5 fusion.16
  1018.3 18.9 copy.122
  1037.1 10.1 all-to-all-start
  1057.4 172.5 %all-to-all-done = f32[2,512,1,4096]{3,0,2,1:T(2,128)} async-done(((f32[2,512,1,4096]{3,0,2,1:T(2,128)}), f32[2,512,1,4096]{3,0,2,1:T(2,128)}, u32[]{:S(2)}, u32[]{:S(2)}) %all-to-all-start) | async-done | bytes 16777248 | tf_op jit(solution)/shard_map/all_to_all | solution.py:63
  1229.8 28.7 copy.192
  1258.6 22.1 reshape.701
  1280.7 21.6 convolution_bitcast_fusion
  1302.3 7.1 subtract_bitcast_fusion.1
  1315.8 80.3 %fusion.21 = f32[2,1,256,16,512]{2,4,3,0,1:T(8,128)} fusion(f32[2,256,16,512]{3,2,1,0:T(8,128)} %maximum_bitcast_fusion.1, f32[1,512,2,512]{1,3,0,2:T(8,128)S(1)} %copy-done, f32[1,512,2,512]{1,3,0,2:T(8,128)S(1)} %get-tuple-element.25), kind=kOutput, calls=%fused_computation.59 | convolution fusion | flops 51540656128 | bytes 37748736 | tf_op jit(solution)/shard_map/pfikc,pcql->qfikl/dot_general | solution.py:50
  1396.1 11.3 copy.125
  1414.2 361.7 %all-to-all-done.1 = f32[2,1,256,16,512]{2,4,0,1,3:T(8,128)} async-done(((f32[2,1,256,16,512]{2,4,0,1,3:T(8,128)}), f32[2,1,256,16,512]{2,4,0,1,3:T(8,128)}, u32[]{:S(2)}, u32[]{:S(2)}) %all-to-all-start.1) | async-done | bytes 16777248 | tf_op jit(solution)/shard_map/all_to_all | solution.py:67
  1775.9 20.3 copy.126
  1796.2 21.6 fusion.24
  1817.7 6.9 subtract_bitcast_fusion
  1828.1 19.3 copy.129
  1847.4 9.7 all-to-all-start.2
  1867.8 172.2 %all-to-all-done.2 = f32[2,16,256,512]{3,2,0,1:T(8,128)} async-done(((f32[2,16,256,512]{3,2,0,1:T(8,128)}), f32[2,16,256,512]{3,2,0,1:T(8,128)}, u32[]{:S(2)}, u32[]{:S(2)}) %all-to-all-start.2) | async-done | bytes 16777248 | tf_op jit(solution)/shard_map/all_to_all | solution.py:63
  2040.1 12.2 copy.130
  2052.3 59.3 %fusion.33 = f32[2,512,8,512,1]{3,1,4,2,0:T(8,128)S(1)} fusion(f32[2,8,512,512,1]{3,2,0,1,4:T(8,128)} %bitcast.232, f32[1,512,2,512]{1,3,0,2:T(8,128)S(1)} %copy-done.1, f32[1,512,2,512]{1,3,0,2:T(8,128)S(1)} %get-tuple-element.25), kind=kOutput, calls=%fused_computation.68 | convolution fusion | flops 51540656128 | bytes 37748736 | tf_op jit(solution)/shard_map/pfmsk,psql->qfmlk/dot_general | solution.py:50
  2117.5 59.5 %fusion.28 = f32[2,512,8,512]{3,1,2,0:T(8,128)S(1)} fusion(f32[1,8,512,512]{3,2,1,0:T(8,128)} %get-tuple-element.12, f32[1,8,512,512]{3,2,1,0:T(8,128)S(1)} %get-tuple-element.11, f32[1,512,2,512]{1,3,2,0:T(8,128)} %get-tuple-element.24, f32[1,512,2,512]{1,3,2,0:T(8,128)S(1)} %copy-done.2), kind=kOutput, calls=%fused_computation.63 | convolution fusion | flops 51544850432 | bytes 37748736 | tf_op jit(solution)/shard_map/pmlk,plqs->qsmk/dot_general | solution.py:50
  2177.0 21.4 copy.134
  2198.4 9.7 all-to-all-start.3
  2208.5 181.7 %all-to-all-done.3 = f32[2,512,8,512]{3,2,0,1:T(8,128)} async-done(((f32[2,512,8,512]{3,2,0,1:T(8,128)}), f32[2,512,8,512]{3,2,0,1:T(8,128)}, u32[]{:S(2)}, u32[]{:S(2)}) %all-to-all-start.3) | async-done | bytes 16777248 | tf_op jit(solution)/shard_map/all_to_all | solution.py:63
  2390.2 6.9 copy.191
  2401.6 19.1 fusion.27
  2420.7 17.7 copy.139
  2443.6 361.8 %all-to-all-done.4 = f32[2,1,256,16,512]{4,2,0,1,3:T(8,128)} async-done(((f32[2,1,256,16,512]{4,2,0,1,3:T(8,128)}), f32[2,1,256,16,512]{4,2,0,1,3:T(8,128)}, u32[]{:S(2)}, u32[]{:S(2)}) %all-to-all-start.4) | async-done | bytes 16777248 | tf_op jit(solution)/shard_map/all_to_all | solution.py:67
  2805.4 57.1 %fusion.18 = f32[2,256,16,512]{1,3,2,0:T(8,128)S(1)} fusion(f32[2,1,256,16,512]{4,2,0,1,3:T(8,128)} %all-to-all-done.4, f32[1,512,2,512]{1,3,2,0:T(8,128)} %get-tuple-element.24, f32[1,512,2,512]{1,3,2,0:T(8,128)S(1)} %copy-done.2), kind=kOutput, calls=%fused_computation.58 | convolution fusion | flops 51540656128 | bytes 37748736 | tf_op jit(solution)/shard_map/pnik,pkqa->qina/dot_general | solution.py:50
  2871.4 20.3 copy.141
  2891.7 13.5 fusion.17
  2905.2 11.8 mul.939
  2917.0 8.3 copy.142
  2925.3 96.1 %all_to_all.90 = f32[256,2,4096]{2,0,1:T(8,128)S(1)} all-to-all(f32[256,2,4096]{2,0,1:T(8,128)S(1)} %copy.142), channel_id=1, replica_groups=mesh['rows'=16,'cols'=2] {'cols'}, dimensions={1} | all-to-all | bytes 16777216 | tf_op jit(solution)/shard_map/all_to_all | solution.py:164
  (60 shorter events, 82.3 us)
Async XLA Ops:
  1.7 27.3 collective-permute-start.1
  3.6 25.4 collective-permute-start
  1037.1 192.7 %all-to-all-start = ((f32[2,512,1,4096]{3,0,2,1:T(2,128)}), f32[2,512,1,4096]{3,0,2,1:T(2,128)}, u32[]{:S(2)}, u32[]{:S(2)}) async-start(f32[2,512,1,4096]{3,0,2,1:T(2,128)} %copy.122), calls=%async_computation | async-start | bytes 33554432 | tf_op jit(solution)/shard_map/all_to_all | solution.py:63
  1309.5 6.4 copy-start
  1407.4 368.4 %all-to-all-start.1 = ((f32[2,1,256,16,512]{2,4,0,1,3:T(8,128)}), f32[2,1,256,16,512]{2,4,0,1,3:T(8,128)}, u32[]{:S(2)}, u32[]{:S(2)}) async-start(f32[2,1,256,16,512]{2,4,0,1,3:T(8,128)} %copy.125), calls=%async_computation.1 | async-start | bytes 33554432 | tf_op jit(solution)/shard_map/all_to_all | solution.py:67
  1847.4 192.7 %all-to-all-start.2 = ((f32[2,16,256,512]{3,2,0,1:T(8,128)}), f32[2,16,256,512]{3,2,0,1:T(8,128)}, u32[]{:S(2)}, u32[]{:S(2)}) async-start(f32[2,16,256,512]{3,2,0,1:T(8,128)} %copy.129), calls=%async_computation.2 | async-start | bytes 33554432 | tf_op jit(solution)/shard_map/all_to_all | solution.py:63
  2040.1 12.2 copy-start.1
  2111.6 5.9 copy-start.2
  2198.4 191.8 %all-to-all-start.3 = ((f32[2,512,8,512]{3,2,0,1:T(8,128)}), f32[2,512,8,512]{3,2,0,1:T(8,128)}, u32[]{:S(2)}, u32[]{:S(2)}) async-start(f32[2,512,8,512]{3,2,0,1:T(8,128)} %copy.134), calls=%async_computation.3 | async-start | bytes 33554432 | tf_op jit(solution)/shard_map/all_to_all | solution.py:63
  2438.4 367.0 %all-to-all-start.4 = ((f32[2,1,256,16,512]{4,2,0,1,3:T(8,128)}), f32[2,1,256,16,512]{4,2,0,1,3:T(8,128)}, u32[]{:S(2)}, u32[]{:S(2)}) async-start(f32[2,1,256,16,512]{4,2,0,1,3:T(8,128)} %copy.139), calls=%async_computation.4 | async-start | bytes 33554432 | tf_op jit(solution)/shard_map/all_to_all | solution.py:67
where the time goes:
time: 3040 us; the launch traced here: 3030 us
  waiting for transfers between devices  1250 us (41%)
  other arithmetic  709 us (23%)
  local copies, waits for them, and re-layouts  592 us (19%)
  matrix products  332 us (11%)
  blocking collectives  96.1 us (3%)
  starting transfers between devices  45.3 us (1%)
    all_to_all x2, waiting for transfers between devices, across_rows(): lax.all_to_all(values, 'rows', split_axis=3, concat_axis=1, tiled=True)  723 us
    reduce_sum x6, other arithmetic, remap_tiles(): pulled = pulled + jnp.sum(window * weights[None, :, :, :, None], axis=1)  545 us
    all_to_all x3, waiting for transfers between devices, across_columns(): lax.all_to_all(values, 'cols', split_axis=1, concat_axis=2, tiled=True)  526 us
    dot_general x7, matrix products, contract_indices(): jnp.einsum(formula, values, matrix, precision=highest, preferred_element_...  318 us
    gather x1, local copies, waits for them, and re-layouts, remap_tiles(): picked = jnp.take(tile_rows, flat_index.reshape(-1), axis=1)  216 us
    all_to_all x1, blocking collectives, per_device(): lax.all_to_all(image, 'cols', split_axis=1, concat_axis=0, tiled=True)  96.1 us
    reshape x2, local copies, waits for them, and re-layouts, remap_tiles(): tile_rows = padded.reshape(2, (rows_dev + 2 * HALO) * tiles_dev, TILE)  74.5 us
  transfers between devices with their start and end apart: 7, of which 5 were waited for; matrix products, arithmetic and copies ran while one was open for 1% of the time, Pallas kernels for 0%

commit v1 on v0

--- a/solution.py
+++ b/solution.py
@@ -1,11 +1,15 @@
 import math
+from functools import partial
 
 import jax
 import jax.numpy as jnp
+import ml_dtypes
+import numpy as np
 from jax import lax
+from jax.experimental import pallas as pl
+from jax.experimental.pallas import tpu as pltpu
 from jax.sharding import PartitionSpec as P
 
-N = 8192
 TILE = 128
 PAIRS = 2
 HALO = 8
@@ -52,11 +56,11 @@
     )
 
 
-def signed_wave(counter):
-    middle = N // 2
-    shifted = jnp.where(counter > middle, counter - N, counter)
+def signed_wave(counter, n):
+    middle = n // 2
+    shifted = jnp.where(counter > middle, counter - n, counter)
     shifted = jnp.where(counter == middle, 0, shifted)
-    return shifted.astype(jnp.float32) * (2.0 * math.pi / N)
+    return shifted.astype(jnp.float32) * (2.0 * math.pi / n)
 
 
 def across_columns(values):
@@ -86,8 +90,8 @@
     return pulled.reshape(2, rows_dev, tiles_dev * TILE)
 
 
-def weigh_spectra(power_spectra, row_wave, col_wave):
-    floored_wavenumber = 8.0 * math.pi / N
+def weigh_spectra(power_spectra, row_wave, col_wave, n):
+    floored_wavenumber = 8.0 * math.pi / n
     weight = local_weight + 1.0 / (
         row_wave * row_wave + col_wave * col_wave + floored_wavenumber * floored_wavenumber
     )
@@ -96,7 +100,617 @@
     return jnp.stack([real_part, imag_part])
 
 
-def per_device(residual, field_slopes, source_tile, row_shift, pixel_shift, fraction):
+GROUP = 16
+SLICES = 4
+STEPS = tuple(range(-SHIFT, SHIFT + 2))
+VMEM_LIMIT = 48 * 2**20
+
+
+def turn(x, numerator, denominator):
+    numerator %= denominator
+    re, im = x
+    if numerator == 0:
+        return x
+    if 4 * numerator == denominator:
+        return (-im, re)
+    if 2 * numerator == denominator:
+        return (-re, -im)
+    if 4 * numerator == 3 * denominator:
+        return (im, -re)
+    if 8 * numerator % denominator == 0:
+        half = math.sqrt(0.5)
+        a, b = half * re, half * im
+        return {1: (a - b, a + b), 3: (-a - b, a - b), 5: (b - a, -a - b), 7: (a + b, b - a)}[
+            8 * numerator // denominator
+        ]
+    angle = 2.0 * math.pi * numerator / denominator
+    c, s = math.cos(angle), math.sin(angle)
+    return (re * c - im * s, re * s + im * c)
+
+
+def dft(xs, sign):
+    n = len(xs)
+    if n == 1:
+        return xs
+    even, odd = dft(xs[0::2], sign), dft(xs[1::2], sign)
+    odd = [turn(x, sign * k, n) for k, x in enumerate(odd)]
+    first = [(e[0] + o[0], e[1] + o[1]) for e, o in zip(even, odd)]
+    second = [(e[0] - o[0], e[1] - o[1]) for e, o in zip(even, odd)]
+    return first + second
+
+
+def staged_dft(load, store, n, sign, hold):
+    outer = 8 if n >= 32 else 2
+    inner = n // outer
+    for a in range(outer):
+        ys = dft([load(a + outer * b) for b in range(inner)], sign)
+        for k, y in enumerate(ys):
+            re, im = turn(y, sign * a * k, n)
+            hold[k * outer + a, 0] = re
+            hold[k * outer + a, 1] = im
+    for k in range(inner):
+        zs = dft([(hold[k * outer + a, 0], hold[k * outer + a, 1]) for a in range(outer)], sign)
+        for b, z in enumerate(zs):
+            store(k + inner * b, z)
+
+
+def split(x):
+    high = x.astype(jnp.bfloat16)
+    return high, (x - high.astype(jnp.float32)).astype(jnp.bfloat16)
+
+
+def product(left, right):
+    dot = lambda a, b: jnp.dot(a, b, preferred_element_type=jnp.float32)
+    return dot(left[0], right[0]) + (dot(left[1], right[0]) + dot(left[0], right[1]))
+
+
+def halves(matrix):
+    high = np.asarray(matrix, np.float32).astype(ml_dtypes.bfloat16)
+    low = (np.asarray(matrix, np.float32) - high.astype(np.float32)).astype(ml_dtypes.bfloat16)
+    return jnp.asarray(high), jnp.asarray(low)
+
+
+def phases(product_of_indices, length):
+    angle = 2.0 * np.pi * (np.asarray(product_of_indices) % length) / length
+    return np.cos(angle), np.sin(angle)
+
+
+class Plan:
+    def __init__(self, devices):
+        self.devices = devices
+        self.tiles = 2 * devices
+        n = self.n = TILE * self.tiles
+        j = np.arange(TILE)
+        c, s = phases(j[:, None] * j[None, :], TILE)
+        back = TILE - 1 - j
+        self.list_a = halves(np.block([[c, -s], [s, c]]))
+        self.list_b = halves(np.block([[c[:, back], -s[:, back]], [s[:, back], c[:, back]]]))
+        self.rows_forward = halves(np.block([[c, s], [-s, c]]))
+        self.rows_inverse = halves(np.block([[c, -s], [s, c]]))
+        scale = 1.0 / (2.0 * n * n)
+        self.cols_inverse = halves(scale * np.block([[c, s], [-s, c]]))
+        low = j < TILE // 2
+        digit_a = np.where(low, j, j - TILE // 2)
+        digit_b = np.where(low, np.where(j == 0, TILE // 2, TILE - j), TILE - 1 - (j - TILE // 2))
+        ca, sa = phases(j[:, None] * digit_a[None, :], TILE)
+        cb, sb = phases(j[:, None] * digit_b[None, :], TILE)
+        blocks = []
+        for mask in (low, ~low):
+            blocks.append(np.concatenate([ca * mask, cb * mask, -sa * mask, -sb * mask], 1))
+            blocks.append(np.concatenate([sa * mask, sb * mask, ca * mask, cb * mask], 1))
+        self.special_forward = halves(np.concatenate(blocks, 0))
+        freq = np.where(low, 0, devices) + self.tiles * digit_a
+        ci, si = phases(freq[:, None] * j[None, :], n)
+        first = np.concatenate([ci * low[:, None], ci * ~low[:, None]], 1)
+        second = np.concatenate([-si * low[:, None], -si * ~low[:, None]], 1)
+        second[0, :TILE] = 1.0 - 2.0 * (j % 2)
+        second[0, TILE:] = 0.0
+        self.special_inverse = halves(2.0 * scale * np.concatenate([first, second], 0))
+        beta = np.arange(self.tiles)
+        tc, ts = phases(beta[:, None] * j[None, :], n)
+        self.col_twiddle = jnp.asarray(np.stack([tc, ts]), jnp.float32)
+        self.row_twiddle = jnp.asarray(np.stack([tc.T, ts.T]), jnp.float32)
+        self.low = low
+        self.digit_a, self.digit_b = digit_a, digit_b
+
+    def wave_of_lists(self, place):
+        j = jnp.arange(TILE, dtype=jnp.int32)
+        usual = place + self.tiles * j
+        other = jnp.asarray(np.where(self.low, 0, self.devices) + self.tiles * self.digit_a, jnp.int32)
+        other_b = (self.n - other) % self.n
+        other_b = other_b.at[0].set(self.n // 2)
+        a = jnp.where(place == 0, other, usual)
+        b = jnp.where(place == 0, other_b, (self.n - usual) % self.n)
+        return signed_wave(jnp.concatenate([a, b]), self.n).reshape(1, 2 * TILE)
+
+
+def whole(shape):
+    return pl.BlockSpec(shape, lambda *_: (0,) * len(shape))
+
+
+def params():
+    return pltpu.CompilerParams(vmem_limit_bytes=VMEM_LIMIT)
+
+
+def remap_kernel(
+    half_ref, above_ref, below_ref, slopes_ref, source_ref, row_ref, pixel_ref, fraction_ref,
+    moves_ref, out_ref, window, picker, picked, moved,
+):
+    tiles = slopes_ref.shape[2] // TILE
+    span = 2 * GROUP
+    count = PAIRS * tiles * GROUP
+    for t in range(tiles):
+        cols = slice(t * TILE, (t + 1) * TILE)
+        for p in range(2):
+            lanes = slice(p * TILE, (p + 1) * TILE)
+            window[t * span : t * span + GROUP, lanes] = above_ref[p, :, cols]
+            window[t * span + GROUP : (t + 1) * span, lanes] = below_ref[p, :, cols]
+    lane = lax.broadcasted_iota(jnp.int32, (GROUP, TILE), 1)
+    down = lax.broadcasted_iota(jnp.int32, (GROUP, tiles), 0)
+    per = TILE // span
+    for k in range(PAIRS):
+        source = source_ref[k]
+        place = (source % per) * span + down + HALO + row_ref[k]
+        block = source // per
+        for t in range(tiles):
+            here = slice((k * tiles + t) * GROUP, (k * tiles + t + 1) * GROUP)
+            hit = jnp.where(place[:, t : t + 1] == lane, 1.0, 0.0).astype(jnp.bfloat16)
+            blk = jnp.broadcast_to(block[:, t : t + 1], (GROUP, TILE))
+            blk = blk.astype(jnp.float32).astype(jnp.bfloat16)
+            for c in range(tiles * span // TILE):
+                picker[here, c * TILE : (c + 1) * TILE] = jnp.where(
+                    blk == jnp.bfloat16(c), hit, jnp.bfloat16(0)
+                )
+    picked[...] = jnp.dot(
+        picker[...], window[...], preferred_element_type=jnp.float32
+    ).astype(jnp.bfloat16)
+    for p in range(2):
+        moved[p * count : (p + 1) * count, :] = jnp.dot(
+            picked[:, p * TILE : (p + 1) * TILE], moves_ref[...],
+            preferred_element_type=jnp.float32,
+        )
+    for t in range(tiles):
+        pulled = [None, None]
+        for k in range(PAIRS):
+            row0 = (k * tiles + t) * GROUP
+            move = jnp.broadcast_to(pixel_ref[k][:, t : t + 1], (GROUP, TILE))
+            blend = jnp.broadcast_to(fraction_ref[k][:, t : t + 1], (GROUP, TILE))
+            rest = 1.0 - blend
+            same = [move == step for step in STEPS[:-2]]
+            for p in range(2):
+                here = slice(p * count + row0, p * count + row0 + GROUP)
+                part = [moved[here, i * TILE : (i + 1) * TILE] for i in range(len(STEPS))]
+                near, far = part[-2], part[-1]
+                for i in range(len(STEPS) - 2):
+                    near = jnp.where(same[i], part[i], near)
+                    far = jnp.where(same[i], part[i + 1], far)
+                term = rest * near + blend * far
+                pulled[p] = term if pulled[p] is None else pulled[p] + term
+        cols = slice(t * TILE, (t + 1) * TILE)
+        slopes = [slopes_ref[i, :, cols].astype(jnp.float32) for i in range(4)]
+        out_ref[0, :, cols] = -(pulled[0] * slopes[0] + pulled[1] * slopes[1])
+        out_ref[1, :, cols] = -(pulled[0] * slopes[2] + pulled[1] * slopes[3])
+
+
+def remap_flow(half, part, parts, padded, slopes, source, row_shift, pixel_shift, fraction):
+    rows, cols = slopes.shape[1:]
+    tiles = cols // TILE
+    run = TILE // parts
+    steps = run // GROUP
+    half_groups = rows // 2 // GROUP
+
+    def group(l, i, half_ref):
+        return half_ref[0] * half_groups + l * (TILE // GROUP) + part * steps + i
+
+    here = lambda l, i, half_ref: (0, group(l, i, half_ref), 0)
+    after = lambda l, i, half_ref: (0, group(l, i, half_ref) + 1, 0)
+    j = np.arange(TILE)
+    moves = np.concatenate([j[:, None] == j[None, :] + step for step in STEPS], axis=1)
+    small = pl.BlockSpec((PAIRS, GROUP, tiles), here)
+    depth = 2 * GROUP * tiles
+    count = PAIRS * GROUP * tiles
+    runs = rows // 2 // TILE
+    return pl.pallas_call(
+        remap_kernel,
+        grid_spec=pltpu.PrefetchScalarGridSpec(
+            num_scalar_prefetch=1,
+            grid=(runs, steps),
+            in_specs=[
+                pl.BlockSpec((2, GROUP, cols), here),
+                pl.BlockSpec((2, GROUP, cols), after),
+                pl.BlockSpec((4, GROUP, cols), here),
+                small, small, small, small,
+                whole(moves.shape),
+            ],
+            out_specs=pl.BlockSpec((2, GROUP, cols), lambda l, i, _: (0, l * steps + i, 0)),
+            scratch_shapes=[
+                pltpu.VMEM((depth, 2 * TILE), jnp.bfloat16),
+                pltpu.VMEM((count, depth), jnp.bfloat16),
+                pltpu.VMEM((count, 2 * TILE), jnp.bfloat16),
+                pltpu.VMEM((2 * count, len(STEPS) * TILE), jnp.float32),
+            ],
+        ),
+        out_shape=jax.ShapeDtypeStruct((2, runs * run, cols), jnp.float32),
+        compiler_params=params(),
+        cost_estimate=pl.CostEstimate(
+            flops=20_000_000 * runs * run, bytes_accessed=40 * runs * run * cols, transcendentals=0
+        ),
+        name="remap",
+    )(half, padded, padded, slopes, source, row_shift, pixel_shift, fraction,
+      jnp.asarray(moves, jnp.bfloat16))
+
+
+def cols_forward_kernel(
+    sign_ref, own_ref, got_ref, twiddle_ref, a_high, a_low, b_high, b_low, s_high, s_low,
+    out_ref, xa_high, xa_low, xb_high, xb_low, hold,
+):
+    devices = out_ref.shape[0]
+    rows = out_ref.shape[1]
+    sign = sign_ref[0]
+
+    def block(r, carry):
+        at = pl.ds(pl.multiple_of(r * GROUP, GROUP), GROUP)
+
+        def put(beta, z):
+            tc, ts = twiddle_ref[0, beta : beta + 1, :], twiddle_ref[1, beta : beta + 1, :]
+            re, im = z[0] * tc + z[1] * ts, z[1] * tc - z[0] * ts
+            if beta < devices:
+                slot, high, low = beta, xa_high, xa_low
+            else:
+                slot, high, low = (2 * devices - beta) % devices, xb_high, xb_low
+            for i, value in enumerate((re, im)):
+                h, l = split(value)
+                high[slot, at, i * TILE : (i + 1) * TILE] = h
+                low[slot, at, i * TILE : (i + 1) * TILE] = l
+
+        def both(t):
+            cols = slice(t * TILE, (t + 1) * TILE)
+            return [(own_ref[p, at, cols], got_ref[p, at, cols]) for p in range(2)]
+
+        def total(t):
+            return tuple(a + b for a, b in both(t))
+
+        def gap(t):
+            return turn(tuple((a - b) * sign for a, b in both(t)), -t, 2 * devices)
+
+        staged_dft(total, lambda k, z: put(2 * k, z), devices, -1, hold)
+        staged_dft(gap, lambda k, z: put(2 * k + 1, z), devices, -1, hold)
+        return carry
+
+    lax.fori_loop(0, rows // GROUP, block, 0)
+    flat = (devices - 1) * rows
+    for i, (high, low, mh, ml) in enumerate(
+        ((xa_high, xa_low, a_high, a_low), (xb_high, xb_low, b_high, b_low))
+    ):
+        left = tuple(x[1:].reshape(flat, 2 * TILE) for x in (high, low))
+        value = product(left, (mh[...], ml[...]))
+        for part in range(2):
+            lanes = slice((2 * part + i) * TILE, (2 * part + i + 1) * TILE)
+            out_ref[1:, :, lanes] = value[:, part * TILE : (part + 1) * TILE].reshape(
+                devices - 1, rows, TILE
+            )
+    left = tuple(
+        jnp.concatenate([xa[0], xb[0]], axis=1)
+        for xa, xb in ((xa_high, xb_high), (xa_low, xb_low))
+    )
+    out_ref[0] = product(left, (s_high[...], s_low[...]))
+
+
+def cols_forward(plan, sign, own, got):
+    rows, cols = own.shape[1:]
+    d = plan.devices
+    step = 2 * GROUP
+    data = pl.BlockSpec((2, step, cols), lambda i: (0, i, 0))
+    square = whole((2 * TILE, 2 * TILE))
+    wide = whole((4 * TILE, 4 * TILE))
+    return pl.pallas_call(
+        cols_forward_kernel,
+        grid=(rows // step,),
+        in_specs=[
+            pl.BlockSpec(memory_space=pltpu.SMEM), data, data, whole(plan.col_twiddle.shape),
+            square, square, square, square, wide, wide,
+        ],
+        out_specs=pl.BlockSpec((d, step, 4 * TILE), lambda i: (0, i, 0)),
+        out_shape=jax.ShapeDtypeStruct((d, rows, 4 * TILE), jnp.float32),
+        scratch_shapes=[pltpu.VMEM((d, step, 2 * TILE), jnp.bfloat16)] * 4
+        + [pltpu.VMEM((d, 2, GROUP, TILE), jnp.float32)],
+        compiler_params=params(),
+        cost_estimate=pl.CostEstimate(
+            flops=4096 * rows * cols, bytes_accessed=32 * rows * cols, transcendentals=0
+        ),
+        name="cols_forward",
+    )(sign, own, got, plan.col_twiddle, *plan.list_a, *plan.list_b, *plan.special_forward)
+
+
+def rows_forward_kernel(x_ref, twiddle_ref, out_ref, hold):
+    tiles, _, lanes = x_ref.shape
+    half = lanes // 2
+    twiddle = (twiddle_ref[0], twiddle_ref[1])
+
+    def load(s):
+        return x_ref[s, :, :half], x_ref[s, :, half:]
+
+    def store(k, z):
+        tc, ts = twiddle[0][:, k : k + 1], twiddle[1][:, k : k + 1]
+        out_ref[k, :, :half] = z[0] * tc + z[1] * ts
+        out_ref[k, :, half:] = z[1] * tc - z[0] * ts
+
+    staged_dft(load, store, tiles, -1, hold)
+
+
+def rows_forward(plan, part, x):
+    tiles, rows, lanes = x.shape
+    step = 8
+    return pl.pallas_call(
+        rows_forward_kernel,
+        grid=(rows // step,),
+        in_specs=[
+            pl.BlockSpec((tiles, step, lanes), lambda i: (0, i, 0)),
+            pl.BlockSpec((2, step, tiles), lambda i: (0, part * (rows // step) + i, 0)),
+        ],
+        out_specs=pl.BlockSpec((tiles, step, lanes), lambda i: (0, i, 0)),
+        out_shape=jax.ShapeDtypeStruct((tiles, rows, lanes), jnp.float32),
+        scratch_shapes=[pltpu.VMEM((tiles, 2, step, lanes // 2), jnp.float32)],
+        compiler_params=params(),
+        cost_estimate=pl.CostEstimate(
+            flops=64 * x.size, bytes_accessed=8 * x.size, transcendentals=0
+        ),
+        name="rows_forward",
+    )(x, plan.row_twiddle)
+
+
+def weigh_kernel(n, parts, *refs):
+    x_refs = refs[:parts]
+    f_high, f_low, g_high, g_low, wave_ref, out_ref = refs[parts:]
+    batch, _, lanes = out_ref.shape
+    half = lanes // 2
+    tiles = n // TILE
+    col_wave = wave_ref[...]
+    floored = 8.0 * math.pi / n
+    col_part = col_wave * col_wave + floored * floored
+    digit = lax.broadcasted_iota(jnp.int32, (TILE, half), 0)
+    for b in range(batch):
+        x = jnp.concatenate(
+            [r[b, :, :half] for r in x_refs] + [r[b, :, half:] for r in x_refs], axis=0
+        )
+        z = product((f_high[...], f_low[...]), split(x))
+        row_wave = signed_wave(pl.program_id(0) * batch + b + tiles * digit, n)
+        weight = local_weight + 1.0 / (row_wave * row_wave + col_part)
+        re, im = z[:TILE], z[TILE:]
+        z = jnp.concatenate(
+            [weight * (col_wave * im - row_wave * re), -weight * (col_wave * re + row_wave * im)],
+            axis=0,
+        )
+        y = product((g_high[...], g_low[...]), split(z))
+        out_ref[b, :, :half] = y[:TILE]
+        out_ref[b, :, half:] = y[TILE:]
+
+
+def weigh(plan, wave, xs):
+    tiles, rows, lanes = xs[0].shape
+    parts = len(xs)
+    batch = 4
+    square = whole((2 * TILE, 2 * TILE))
+    return pl.pallas_call(
+        partial(weigh_kernel, plan.n, parts),
+        grid=(tiles // batch,),
+        in_specs=[pl.BlockSpec((batch, rows, lanes), lambda i: (i, 0, 0))] * parts
+        + [square] * 4 + [whole(wave.shape)],
+        out_specs=pl.BlockSpec((batch, parts * rows, lanes), lambda i: (i, 0, 0)),
+        out_shape=jax.ShapeDtypeStruct((tiles, parts * rows, lanes), jnp.float32),
+        compiler_params=params(),
+        cost_estimate=pl.CostEstimate(
+            flops=4096 * parts * xs[0].size, bytes_accessed=8 * parts * xs[0].size, transcendentals=0
+        ),
+        name="weigh",
+    )(*xs, *plan.rows_forward, *plan.rows_inverse, wave)
+
+
+def rows_inverse_kernel(x_ref, twiddle_ref, special_ref, out_ref, hold):
+    tiles, _, lanes = x_ref.shape
+    half = lanes // 2
+    twiddle = (twiddle_ref[0], twiddle_ref[1])
+    special = special_ref[...] > 0.5
+
+    def load(k):
+        tc, ts = twiddle[0][:, k : k + 1], twiddle[1][:, k : k + 1]
+        re, im = x_ref[k, :, :half], x_ref[k, :, half:]
+        return re * tc - im * ts, im * tc + re * ts
+
+    def store(s, z):
+        re_a, re_b = z[0][:, :TILE], z[0][:, TILE:]
+        im_a, im_b = z[1][:, :TILE], z[1][:, TILE:]
+        out_ref[s, :, :TILE] = jnp.where(special, re_a, re_a + re_b)
+        out_ref[s, :, TILE:] = jnp.where(special, re_b, im_a - im_b)
+
+    staged_dft(load, store, tiles, 1, hold)
+
+
+def rows_inverse(plan, part, parts, special, x):
+    tiles, rows, lanes = x.shape
+    step = 8
+    run = rows // parts // step
+    return pl.pallas_call(
+        rows_inverse_kernel,
+        grid=(run,),
+        in_specs=[
+            pl.BlockSpec((tiles, step, lanes), lambda i: (0, part * run + i, 0)),
+            pl.BlockSpec((2, step, tiles), lambda i: (0, part * run + i, 0)),
+            whole(special.shape),
+        ],
+        out_specs=pl.BlockSpec((tiles, step, lanes // 2), lambda i: (0, i, 0)),
+        out_shape=jax.ShapeDtypeStruct((tiles, rows // parts, lanes // 2), jnp.float32),
+        scratch_shapes=[pltpu.VMEM((tiles, 2, step, lanes // 2), jnp.float32)],
+        compiler_params=params(),
+        cost_estimate=pl.CostEstimate(
+            flops=64 * x.size // parts, bytes_accessed=6 * x.size // parts, transcendentals=0
+        ),
+        name="rows_inverse",
+    )(x, plan.row_twiddle, special)
+
+
+def cols_inverse_kernel(
+    col_ref, sign_ref, x_ref, twiddle_ref, g_high, g_low, s_high, s_low, *rest,
+):
+    keep_ref, send_ref, spectrum, hold = rest[-4:]
+    devices, rows, _ = x_ref.shape
+    flat = (devices - 1) * rows
+    value = product(split(x_ref[1:].reshape(flat, 2 * TILE)), (g_high[...], g_low[...]))
+    spectrum[1:] = value.reshape(devices - 1, rows, 2 * TILE)
+    spectrum[0] = product(split(x_ref[0]), (s_high[...], s_low[...]))
+    sign = sign_ref[0]
+
+    def block(r, carry):
+        at = pl.ds(pl.multiple_of(r * GROUP, GROUP), GROUP)
+
+        def point(k):
+            tc, ts = twiddle_ref[0, k : k + 1, :], twiddle_ref[1, k : k + 1, :]
+            if k % 2:
+                tc, ts = tc * sign, ts * sign
+            re, im = spectrum[k, at, :TILE], spectrum[k, at, TILE:]
+            return re * tc - im * ts, im * tc + re * ts
+
+        def load(k):
+            if k == 0:
+                p, q = spectrum[0, at, :TILE], spectrum[0, at, TILE:]
+                return p + q, p - q
+            (a, b), (c, d) = point(k), point(devices - k)
+            odd = turn((a - c, b + d), k, 2 * devices)
+            return a + c - odd[1], b - d + odd[0]
+
+        def store(n, z):
+            for i in range(2):
+                t = 2 * n + i
+                ref = keep_ref if t < devices else send_ref
+                t %= devices
+                ref[at, t * TILE : (t + 1) * TILE] = z[i]
+
+        staged_dft(load, store, devices, 1, hold)
+        return carry
+
+    lax.fori_loop(0, rows // GROUP, block, 0)
+
+
+def place_block(part, parts, half_rows, step):
+    run = TILE // parts // step
+    return lambda l, i, half_ref: (
+        half_ref[0] * (half_rows // step) + l * (TILE // step) + part * run + i, 0
+    )
+
+
+def cols_inverse(plan, part, parts, half, sign, x, shape, image):
+    d, rows, _ = x.shape
+    step = min(2 * GROUP, TILE // parts)
+    runs = rows * parts // TILE
+    per = TILE // parts // step
+    cols = shape[1]
+    square = whole((2 * TILE, 2 * TILE))
+    smem = pl.BlockSpec(memory_space=pltpu.SMEM)
+    extra = [] if image is None else [image]
+    return pl.pallas_call(
+        cols_inverse_kernel,
+        grid_spec=pltpu.PrefetchScalarGridSpec(
+            num_scalar_prefetch=1,
+            grid=(runs, per),
+            in_specs=[
+                smem, pl.BlockSpec((d, step, 2 * TILE), lambda l, i, _: (0, l * per + i, 0)),
+                whole(plan.col_twiddle.shape), square, square, square, square,
+            ] + [pl.BlockSpec(memory_space=pl.ANY)] * len(extra),
+            out_specs=[
+                pl.BlockSpec((step, cols), place_block(part, parts, shape[0] // 2, step)),
+                pl.BlockSpec((step, cols), lambda l, i, _: (l * per + i, 0)),
+            ],
+            scratch_shapes=[
+                pltpu.VMEM((d, step, 2 * TILE), jnp.float32),
+                pltpu.VMEM((d, 2, GROUP, TILE), jnp.float32),
+            ],
+        ),
+        out_shape=[
+            jax.ShapeDtypeStruct(shape, jnp.float32),
+            jax.ShapeDtypeStruct((rows, cols), jnp.float32),
+        ],
+        input_output_aliases={8: 0} if extra else {},
+        compiler_params=params(),
+        cost_estimate=pl.CostEstimate(
+            flops=2048 * x.size, bytes_accessed=8 * x.size, transcendentals=0
+        ),
+        name="cols_inverse",
+    )(half, sign, x, plan.col_twiddle, *plan.cols_inverse, *plan.special_inverse, *extra)
+
+
+def place_kernel(half_ref, got_ref, image_ref, out_ref):
+    out_ref[...] = got_ref[...]
+
+
+def place_rows(part, parts, half, got, image):
+    rows, cols = got.shape
+    step = min(2 * GROUP, TILE // parts)
+    runs = rows * parts // TILE
+    per = TILE // parts // step
+    return pl.pallas_call(
+        place_kernel,
+        grid_spec=pltpu.PrefetchScalarGridSpec(
+            num_scalar_prefetch=1,
+            grid=(runs, per),
+            in_specs=[
+                pl.BlockSpec((step, cols), lambda l, i, _: (l * per + i, 0)),
+                pl.BlockSpec(memory_space=pl.ANY),
+            ],
+            out_specs=pl.BlockSpec(
+                (step, cols), place_block(part, parts, image.shape[0] // 2, step)
+            ),
+        ),
+        out_shape=jax.ShapeDtypeStruct(image.shape, jnp.float32),
+        input_output_aliases={2: 0},
+        compiler_params=params(),
+        cost_estimate=pl.CostEstimate(flops=0, bytes_accessed=8 * got.size, transcendentals=0),
+        name="place_rows",
+    )(half, got, image)
+
+
+def paired(residual, field_slopes, source_tile, row_shift, pixel_shift, fraction):
+    rows_dev, cols_dev = residual.shape[1:]
+    devices = lax.axis_size("rows") * lax.axis_size("cols")
+    plan = Plan(devices)
+    parts = SLICES
+    col = lax.axis_index("cols").astype(jnp.int32)
+    place = lax.axis_index("rows").astype(jnp.int32) * 2 + col
+    mine, other = col.reshape(1), (1 - col).reshape(1)
+    sign = (1 - 2 * col).astype(jnp.float32).reshape(1)
+    swap = [(0, 1), (1, 0)]
+    both = ("rows", "cols")
+    padded = with_halo(residual, (("rows", 1),), HALO)
+    args = (padded, field_slopes, source_tile, row_shift, pixel_shift, fraction)
+    lane = jnp.arange(TILE, dtype=jnp.int32).reshape(1, TILE)
+    special = jnp.where((lane == 0) & (place == 0), 1.0, 0.0)
+    wave = plan.wave_of_lists(place)
+    spectra = []
+    for m in range(parts):
+        away = remap_flow(other, m, parts, *args)
+        got = lax.ppermute(away, "cols", swap)
+        own = remap_flow(mine, m, parts, *args)
+        lists = cols_forward(plan, sign, own, got)
+        lists = lax.all_to_all(lists, both, split_axis=0, concat_axis=0, tiled=True)
+        rows = lists.shape[1]
+        lists = lists.reshape(2 * devices, rows // 2, 4 * TILE)
+        spectra.append(rows_forward(plan, m, lists))
+    mixed = weigh(plan, wave, spectra)
+    image = None
+    sent = []
+    for m in range(parts):
+        folded = rows_inverse(plan, m, parts, special, mixed)
+        folded = folded.reshape(devices, 2 * folded.shape[1], 2 * TILE)
+        folded = lax.all_to_all(folded, both, split_axis=0, concat_axis=0, tiled=True)
+        image, away = cols_inverse(
+            plan, m, parts, mine, sign, folded, (rows_dev, cols_dev), image
+        )
+        sent.append(lax.ppermute(away, "cols", swap))
+    for m in range(parts):
+        image = place_rows(m, parts, other, sent[m], image)
+    return image
+
+
+def general(residual, field_slopes, source_tile, row_shift, pixel_shift, fraction):
     padded = with_halo(residual, (("rows", 1),), HALO)
     pulled = remap_tiles(padded, source_tile, row_shift, pixel_shift, fraction)
     slopes = field_slopes.astype(jnp.float32)
@@ -107,6 +721,7 @@
     rows_count = lax.axis_size("rows")
     cols_count = lax.axis_size("cols")
     part_rows = rows_dev // cols_count
+    n = rows_dev * rows_count
     spread = rows_count // cols_count
     col_index = lax.axis_index("cols")
     row_place = lax.axis_index("rows")
@@ -122,15 +737,15 @@
     power_spectra = contract_indices("pibc,pbqk->qikc", stacked_planes, compact_forward_transform)[
         :, None
     ]
-    cosine, sine_part = phase_pair(wave_index[:, None] * pixel_index[None, :], N, -1)
+    cosine, sine_part = phase_pair(wave_index[:, None] * pixel_index[None, :], n, -1)
     power_spectra = rotate(power_spectra, cosine, sine_part)
     power_spectra = contract_indices("pfikc,pcql->qfikl", power_spectra, large_forward)
     fields = power_spectra.shape[1]
-    back_cos, back_sin = phase_pair(wave_index[:, None] * pixel_index[None, :], N, 1)
+    back_cos, back_sin = phase_pair(wave_index[:, None] * pixel_index[None, :], n, 1)
     power_spectra = across_rows(power_spectra)
     power_spectra = power_spectra.reshape(2, fields, rows_count, part_rows, rows_dev)
     power_spectra = contract_indices("pfrik,prqm->qfmik", power_spectra, compact_forward_transform)
-    band_cos, band_sin = phase_pair(wave_index[:, None] * band[None, :], N, -1)
+    band_cos, band_sin = phase_pair(wave_index[:, None] * band[None, :], n, -1)
     power_spectra = rotate(power_spectra, band_cos[:, :, None], band_sin[:, :, None])
     power_spectra = across_columns(
         power_spectra.reshape(2 * fields, rows_count, part_rows, rows_dev)
@@ -141,12 +756,12 @@
         rows_count * pixel_index[None, :]
         + (col_index * spread + jnp.arange(spread, dtype=jnp.int32))[:, None]
     )
-    row_wave = signed_wave(row_freq)[:, :, None]
-    col_wave = signed_wave(rows_count * pixel_index + row_place)
-    mixed = weigh_spectra(power_spectra, row_wave, col_wave)
+    row_wave = signed_wave(row_freq, n)[:, :, None]
+    col_wave = signed_wave(rows_count * pixel_index + row_place, n)
+    mixed = weigh_spectra(power_spectra, row_wave, col_wave, n)
     mixed = contract_indices("pmlk,plqs->qsmk", mixed, large_inverse)
     mixed = across_columns(mixed)
-    band_cos, band_sin = phase_pair(band[:, None] * wave_index[None, :], N, 1)
+    band_cos, band_sin = phase_pair(band[:, None] * wave_index[None, :], n, 1)
     mixed = rotate(mixed, band_cos[:, :, None], band_sin[:, :, None])
     mixed = contract_indices("pimk,pmqr->qirk", mixed, compact_inverse_transform)
     mixed = across_rows(mixed.reshape(2, 1, part_rows, rows_count, rows_dev))
@@ -160,10 +775,19 @@
         precision=highest,
         preferred_element_type=jnp.float32,
     )
-    image = image.reshape(part_rows, cols_count, cols_dev) * (1.0 / (N * N))
+    image = image.reshape(part_rows, cols_count, cols_dev) * (1.0 / (n * n))
     return lax.all_to_all(image, "cols", split_axis=1, concat_axis=0, tiled=True).reshape(
         rows_dev, cols_dev
     )
+
+
+def per_device(*arrays):
+    rows_dev, cols_dev = arrays[0].shape[1:]
+    rows_count, cols_count = lax.axis_size("rows"), lax.axis_size("cols")
+    devices = rows_count * cols_count
+    if cols_count == 2 and rows_dev * rows_count == cols_dev * cols_count == 2 * TILE * devices:
+        return paired(*arrays)
+    return general(*arrays)
 
 
 def solution(mesh):

time: 3040 us -> 836 us (0.28)
  waiting for transfers between devices: 1250 us -> 507 us
  other arithmetic: 709 us -> 0.03 us
  local copies, waits for them, and re-layouts: 592 us -> 29.8 us
  matrix products: 332 us -> 0 us
  Pallas kernels: 0 us -> 222 us
  blocking collectives: 96.1 us -> 0 us
    all_to_all x5 -> x8, waiting for transfers between devices: 1250 us -> 223 us  [the longest x4 152 us: paired(): lax.all_to_all(folded, both, split_axis=0, concat_axis=0, tiled=True)]
    reduce_sum x6 -> x0, other arithmetic: 545 us -> none  [remap_tiles(): pulled = pulled + jnp.sum(window * weights[None, :, :, :, None], axis=1)]
    dot_general x8 -> x0, matrix products: 332 us -> none  [the longest x7 318 us: contract_indices(): jnp.einsum(formula, values, matrix, precision=highest, preferred_element_...]
    ppermute x0 -> x8, waiting for transfers between devices: none -> 284 us  [the longest x4 222 us: paired(): got = lax.ppermute(away, 'cols', swap)]
    pallas_call x0 -> x29, Pallas kernels: none -> 222 us  [the longest x8 110 us: remap_flow(): pl.pallas_call(remap_kernel, grid_spec=pltpu.PrefetchScalarGridSpec(num_s...]
    gather x1 -> x0, local copies, waits for them, and re-layouts: 216 us -> none  [remap_tiles(): picked = jnp.take(tile_rows, flat_index.reshape(-1), axis=1)]
    reshape x7 -> x0, local copies, waits for them, and re-layouts: 153 us -> none  [the longest x2 74.5 us: remap_tiles(): tile_rows = padded.reshape(2, (rows_dev + 2 * HALO) * tiles_dev, TILE)]
    all_to_all x1 -> x0, blocking collectives: 96.1 us -> none  [per_device(): lax.all_to_all(image, 'cols', split_axis=1, concat_axis=0, tiled=True)]
  transfers between devices with their start and end apart: 7 -> 18, of which waited for: 5 -> 11; matrix products, arithmetic and copies ran while one was open for 1% -> 2% of each run, Pallas kernels for 0% -> 20%
where the time goes in v1:
time: 836 us; the launch traced here: 828 us
  waiting for transfers between devices  507 us (61%)
  Pallas kernels  222 us (27%)
  starting transfers between devices  68.1 us (8%)
  local copies, waits for them, and re-layouts  29.8 us (4%)
    ppermute x4, waiting for transfers between devices, paired(): got = lax.ppermute(away, 'cols', swap)  222 us
    all_to_all x4, waiting for transfers between devices, paired(): lax.all_to_all(folded, both, split_axis=0, concat_axis=0, tiled=True)  152 us
    pallas_call x8, Pallas kernels, remap_flow(): pl.pallas_call(remap_kernel, grid_spec=pltpu.PrefetchScalarGridSpec(num_s...  110 us
    all_to_all x4, waiting for transfers between devices, paired(): lists = lax.all_to_all(lists, both, split_axis=0, concat_axis=0, tiled=True)  71.6 us
    ppermute x4, waiting for transfers between devices, paired(): sent.append(lax.ppermute(away, 'cols', swap))  61.4 us
    unnamed x84, local copies, waits for them, and re-layouts  28.1 us
    pallas_call x4, Pallas kernels, cols_forward(): pl.pallas_call(cols_forward_kernel, grid=(rows // step,), in_specs=[pl.Bl...  27.6 us
    all_to_all x4, starting transfers between devices, paired(): lists = lax.all_to_all(lists, both, split_axis=0, concat_axis=0, tiled=True)  26.7 us
  transfers between devices with their start and end apart: 18, of which 11 were waited for; matrix products, arithmetic and copies ran while one was open for 2% of the time, Pallas kernels for 20%

profile of v1, /device:TPU:12, one launch (start us, length us, event | category | flops | bytes accessed | tf_op | source)
XLA Modules:
  0.0 828.0 jit_solution(4508277147346165696)
XLA Ops:
  2.9 3.6 collective-permute-start.1
  11.7 7.9 constant_dynamic-update-slice_fusion.1
  20.2 14.3 %remap.9 = f32[2,64,4096]{2,1,0:T(8,128)} custom-call(s32[1]{0:T(128)} %bitcast.half_ref, bf16[2,528,4096]{2,1,0:T(8,128)(2,1)} %constant_dynamic-update-slice_fusion.above_ref.below_ref, bf16[2,528,4096]{2,1,0:T(8,128)(2,1)} %constant_dynamic-update-slice_fusion.above_ref.below_ref, bf16[4,512,4096]{2,1,0:T(8,128)(2,1)} %slopes_ref.15, ...), custom_call_target="tpu_custom_call" | custom-call | flops 1280000000 | bytes 10485760 | tf_op jit(solution)/shard_map/remap/pallas_call | solution.py:313
  36.1 13.8 %remap.8.own_ref = f32[2,64,4096]{2,1,0:T(8,128)S(1)} custom-call(s32[1]{0:T(128)} %bitcast.1.half_ref.col_ref, bf16[2,528,4096]{2,1,0:T(8,128)(2,1)} %constant_dynamic-update-slice_fusion.above_ref.below_ref, bf16[2,528,4096]{2,1,0:T(8,128)(2,1)} %constant_dynamic-update-slice_fusion.above_ref.below_ref, bf16[4,512,4096]{2,1,0:T(8,128)(2,1)} %slopes_ref.15, ...), custom_call_target="tpu_custom_call" | custom-call | flops 1280000000 | bytes 10485760 | tf_op jit(solution)/shard_map/remap/pallas_call | solution.py:313
  49.9 32.4 %collective-permute-done.2.got_ref = f32[2,64,4096]{2,1,0:T(8,128)} collective-permute-done((f32[2,64,4096]{2,1,0:T(8,128)}, f32[2,64,4096]{2,1,0:T(8,128)}, u32[]{:S(2)}, u32[]{:S(2)}) %collective-permute-start.2) | collective-permute-done | bytes 2097184 | tf_op jit(solution)/shard_map/ppermute | solution.py:690
  82.4 7.6 cols_forward.4
  90.0 5.8 all-to-all-start
  95.8 13.7 %remap.11 = f32[2,64,4096]{2,1,0:T(8,128)S(1)} custom-call(s32[1]{0:T(128)} %bitcast.half_ref, bf16[2,528,4096]{2,1,0:T(8,128)(2,1)} %constant_dynamic-update-slice_fusion.above_ref.below_ref, bf16[2,528,4096]{2,1,0:T(8,128)(2,1)} %constant_dynamic-update-slice_fusion.above_ref.below_ref, bf16[4,512,4096]{2,1,0:T(8,128)(2,1)} %slopes_ref.15, ...), custom_call_target="tpu_custom_call" | custom-call | flops 1280000000 | bytes 10485760 | tf_op jit(solution)/shard_map/remap/pallas_call | solution.py:313
  111.1 13.6 %remap.10.own_ref = f32[2,64,4096]{2,1,0:T(8,128)S(1)} custom-call(s32[1]{0:T(128)} %bitcast.1.half_ref.col_ref, bf16[2,528,4096]{2,1,0:T(8,128)(2,1)} %constant_dynamic-update-slice_fusion.above_ref.below_ref, bf16[2,528,4096]{2,1,0:T(8,128)(2,1)} %constant_dynamic-update-slice_fusion.above_ref.below_ref, bf16[4,512,4096]{2,1,0:T(8,128)(2,1)} %slopes_ref.15, ...), custom_call_target="tpu_custom_call" | custom-call | flops 1280000000 | bytes 10485760 | tf_op jit(solution)/shard_map/remap/pallas_call | solution.py:313
  124.7 63.4 %collective-permute-done.3.got_ref = f32[2,64,4096]{2,1,0:T(8,128)S(1)} collective-permute-done((f32[2,64,4096]{2,1,0:T(8,128)S(1)}, f32[2,64,4096]{2,1,0:T(8,128)S(1)}, u32[]{:S(2)}, u32[]{:S(2)}) %collective-permute-start.3) | collective-permute-done | bytes 2097184 | tf_op jit(solution)/shard_map/ppermute | solution.py:690
  188.1 6.7 cols_forward.5
  194.8 7.1 all-to-all-start.1
  201.8 13.7 %remap.13 = f32[2,64,4096]{2,1,0:T(8,128)S(1)} custom-call(s32[1]{0:T(128)} %bitcast.half_ref, bf16[2,528,4096]{2,1,0:T(8,128)(2,1)} %constant_dynamic-update-slice_fusion.above_ref.below_ref, bf16[2,528,4096]{2,1,0:T(8,128)(2,1)} %constant_dynamic-update-slice_fusion.above_ref.below_ref, bf16[4,512,4096]{2,1,0:T(8,128)(2,1)} %slopes_ref.15, ...), custom_call_target="tpu_custom_call" | custom-call | flops 1280000000 | bytes 10485760 | tf_op jit(solution)/shard_map/remap/pallas_call | solution.py:313
  217.1 13.6 %remap.12.own_ref = f32[2,64,4096]{2,1,0:T(8,128)S(1)} custom-call(s32[1]{0:T(128)} %bitcast.1.half_ref.col_ref, bf16[2,528,4096]{2,1,0:T(8,128)(2,1)} %constant_dynamic-update-slice_fusion.above_ref.below_ref, bf16[2,528,4096]{2,1,0:T(8,128)(2,1)} %constant_dynamic-update-slice_fusion.above_ref.below_ref, bf16[4,512,4096]{2,1,0:T(8,128)(2,1)} %slopes_ref.15, ...), custom_call_target="tpu_custom_call" | custom-call | flops 1280000000 | bytes 10485760 | tf_op jit(solution)/shard_map/remap/pallas_call | solution.py:313
  230.8 63.4 %collective-permute-done.4.got_ref = f32[2,64,4096]{2,1,0:T(8,128)S(1)} collective-permute-done((f32[2,64,4096]{2,1,0:T(8,128)S(1)}, f32[2,64,4096]{2,1,0:T(8,128)S(1)}, u32[]{:S(2)}, u32[]{:S(2)}) %collective-permute-start.4) | collective-permute-done | bytes 2097184 | tf_op jit(solution)/shard_map/ppermute | solution.py:690
  294.1 6.6 cols_forward.6
  300.8 7.1 all-to-all-start.2
  307.9 13.7 %remap.15 = f32[2,64,4096]{2,1,0:T(8,128)S(1)} custom-call(s32[1]{0:T(128)} %bitcast.half_ref, bf16[2,528,4096]{2,1,0:T(8,128)(2,1)} %constant_dynamic-update-slice_fusion.above_ref.below_ref, bf16[2,528,4096]{2,1,0:T(8,128)(2,1)} %constant_dynamic-update-slice_fusion.above_ref.below_ref, bf16[4,512,4096]{2,1,0:T(8,128)(2,1)} %slopes_ref.15, ...), custom_call_target="tpu_custom_call" | custom-call | flops 1280000000 | bytes 10485760 | tf_op jit(solution)/shard_map/remap/pallas_call | solution.py:313
  323.2 13.6 %remap.14.own_ref = f32[2,64,4096]{2,1,0:T(8,128)S(1)} custom-call(s32[1]{0:T(128)} %bitcast.1.half_ref.col_ref, bf16[2,528,4096]{2,1,0:T(8,128)(2,1)} %constant_dynamic-update-slice_fusion.above_ref.below_ref, bf16[2,528,4096]{2,1,0:T(8,128)(2,1)} %constant_dynamic-update-slice_fusion.above_ref.below_ref, bf16[4,512,4096]{2,1,0:T(8,128)(2,1)} %slopes_ref.15, ...), custom_call_target="tpu_custom_call" | custom-call | flops 1280000000 | bytes 10485760 | tf_op jit(solution)/shard_map/remap/pallas_call | solution.py:313
  336.8 63.4 %collective-permute-done.5.got_ref = f32[2,64,4096]{2,1,0:T(8,128)S(1)} collective-permute-done((f32[2,64,4096]{2,1,0:T(8,128)S(1)}, f32[2,64,4096]{2,1,0:T(8,128)S(1)}, u32[]{:S(2)}, u32[]{:S(2)}) %collective-permute-start.5) | collective-permute-done | bytes 2097184 | tf_op jit(solution)/shard_map/ppermute | solution.py:690
  400.2 6.7 cols_forward.7
  406.8 6.7 all-to-all-start.3
  413.7 4.3 rows_forward.4.refs_0_
  420.0 4.3 rows_forward.5.refs_1_
  426.3 4.3 rows_forward.6.refs_2_
  432.6 71.6 %all-to-all-done.3 = f32[32,64,512]{2,1,0:T(8,128)} async-done(((f32[32,64,512]{2,1,0:T(8,128)}), f32[32,64,512]{2,1,0:T(8,128)}, u32[]{:S(2)}, u32[]{:S(2)}) %all-to-all-start.3) | async-done | bytes 4194336 | tf_op jit(solution)/shard_map/all_to_all | solution.py:693
  504.2 4.4 rows_forward.7.refs_3_
  508.7 2.1 copy-done.13
  510.8 25.4 %weigh.1.x_ref = f32[64,128,512]{2,1,0:T(8,128)} custom-call(f32[64,32,512]{2,1,0:T(8,128)S(1)} %copy-done.10, f32[64,32,512]{2,1,0:T(8,128)} %copy-done.11, f32[64,32,512]{2,1,0:T(8,128)} %copy-done.12, f32[64,32,512]{2,1,0:T(8,128)} %copy-done.13, bf16[256,256]{1,0:T(8,128)(2,1)S(1)} %copy-done.36, bf16[256,256]{1,0:T(8,128)(2,1)S(1)} %copy-done.35, ...), custom_call_target="tpu_custom_call" | custom-call | flops 17179869184 | bytes 33554432 | tf_op jit(solution)/shard_map/weigh/pallas_call | solution.py:494
  536.2 5.3 rows_inverse.7
  541.5 8.3 %all-to-all-start.7 = ((f32[32,64,256]{2,1,0:T(8,128)}), f32[32,64,256]{2,1,0:T(8,128)S(1)}, u32[]{:S(2)}, u32[]{:S(2)}) async-start(f32[32,64,256]{2,1,0:T(8,128)} %bitcast.12), calls=%async_computation.7 | async-start | bytes 4194304 | tf_op jit(solution)/shard_map/all_to_all | solution.py:703
  549.8 4.5 rows_inverse.6
  555.6 40.6 %all-to-all-done.7.x_ref = f32[32,64,256]{2,1,0:T(8,128)S(1)} async-done(((f32[32,64,256]{2,1,0:T(8,128)}), f32[32,64,256]{2,1,0:T(8,128)S(1)}, u32[]{:S(2)}, u32[]{:S(2)}) %all-to-all-start.7) | async-done | bytes 2097184 | tf_op jit(solution)/shard_map/all_to_all | solution.py:703
  597.6 5.8 all-to-all-start.6
  603.4 4.5 rows_inverse.5
  609.2 40.8 %all-to-all-done.6.x_ref = f32[32,64,256]{2,1,0:T(8,128)S(1)} async-done(((f32[32,64,256]{2,1,0:T(8,128)}), f32[32,64,256]{2,1,0:T(8,128)S(1)}, u32[]{:S(2)}, u32[]{:S(2)}) %all-to-all-start.6) | async-done | bytes 2097184 | tf_op jit(solution)/shard_map/all_to_all | solution.py:703
  650.0 5.9 all-to-all-start.5
  655.9 4.5 rows_inverse.4
  661.8 40.8 %all-to-all-done.5.x_ref = f32[32,64,256]{2,1,0:T(8,128)} async-done(((f32[32,64,256]{2,1,0:T(8,128)}), f32[32,64,256]{2,1,0:T(8,128)}, u32[]{:S(2)}, u32[]{:S(2)}) %all-to-all-start.5) | async-done | bytes 2097184 | tf_op jit(solution)/shard_map/all_to_all | solution.py:703
  702.6 5.8 all-to-all-start.4
  710.0 3.7 cols_inverse.4
  713.7 3.7 cols_inverse.5
  717.4 4.7 cols_inverse.6
  725.6 29.5 %all-to-all-done.4.x_ref = f32[32,64,256]{2,1,0:T(8,128)S(1)} async-done(((f32[32,64,256]{2,1,0:T(8,128)}), f32[32,64,256]{2,1,0:T(8,128)S(1)}, u32[]{:S(2)}, u32[]{:S(2)}) %all-to-all-start.4) | async-done | bytes 2097184 | tf_op jit(solution)/shard_map/all_to_all | solution.py:703
  755.1 3.5 cols_inverse.7
  759.1 45.6 %collective-permute-done.9.got_ref = f32[64,4096]{1,0:T(8,128)} collective-permute-done((f32[64,4096]{1,0:T(8,128)}, f32[64,4096]{1,0:T(8,128)}, u32[]{:S(2)}, u32[]{:S(2)}) %collective-permute-start.9) | collective-permute-done | bytes 1048608 | tf_op jit(solution)/shard_map/ppermute | solution.py:707
  806.8 2.0 place_rows.5.image_ref
  810.8 15.9 %collective-permute-done.6.got_ref = f32[64,4096]{1,0:T(8,128)S(1)} collective-permute-done((f32[64,4096]{1,0:T(8,128)S(1)}, f32[64,4096]{1,0:T(8,128)S(1)}, u32[]{:S(2)}, u32[]{:S(2)}) %collective-permute-start.6) | collective-permute-done | bytes 1048608 | tf_op jit(solution)/shard_map/ppermute | solution.py:707
  (106 shorter events, 36.9 us)
Async XLA Ops:
  1.0 10.0 %collective-permute-start = (bf16[2,8,4096]{2,1,0:T(8,128)(2,1)S(1)}, bf16[2,8,4096]{2,1,0:T(8,128)(2,1)S(1)}, u32[]{:S(2)}, u32[]{:S(2)}) collective-permute-start(bf16[2,8,4096]{2,1,0:T(8,128)(2,1)S(1)} %get-tuple-element.34), channel_id=1, source_target_pairs={{0,2},{2,4},{4,6},{6,8},{8,10},{10,12},{12,14},{14,16},{16,18},{18... | collective-permute-start | bytes 393224 | tf_op jit(solution)/shard_map/ppermute | solution.py:30
  2.9 16.6 %collective-permute-start.1 = (bf16[2,8,4096]{2,1,0:T(8,128)(2,1)S(1)}, bf16[2,8,4096]{2,1,0:T(8,128)(2,1)S(1)}, u32[]{:S(2)}, u32[]{:S(2)}) collective-permute-start(bf16[2,8,4096]{2,1,0:T(8,128)(2,1)S(1)} %get-tuple-element.33), channel_id=1, source_target_pairs={{2,0},{4,2},{6,4},{8,6},{10,8},{12,10},{14,12},{16,14},{18,16},{20... | collective-permute-start | bytes 393224 | tf_op jit(solution)/shard_map/ppermute | solution.py:31
  11.7 8.6 %copy-start = (bf16[128,768]{1,0:T(8,128)(2,1)S(1)}, bf16[128,768]{1,0:T(8,128)(2,1)}, u32[]{:S(2)}) copy-start(bf16[128,768]{1,0:T(8,128)(2,1)} %constant.120.clone.moves_ref) | copy-start | bytes 589828
  34.6 47.8 %collective-permute-start.2 = (f32[2,64,4096]{2,1,0:T(8,128)}, f32[2,64,4096]{2,1,0:T(8,128)}, u32[]{:S(2)}, u32[]{:S(2)}) collective-permute-start(f32[2,64,4096]{2,1,0:T(8,128)} %remap.9), channel_id=1, source_target_pairs={{0,1},{1,0},{2,3},{3,2},{4,5},{5,4},{6,7},{7,6},{8,9},{9,8},{10,11... | collective-permute-start | bytes 6291464 | tf_op jit(solution)/shard_map/ppermute | solution.py:690
  36.0 46.3 %copy-start.2 = (bf16[512,512]{1,0:T(8,128)(2,1)S(1)}, bf16[512,512]{1,0:T(8,128)(2,1)}, u32[]{:S(2)}) copy-start(bf16[512,512]{1,0:T(8,128)(2,1)} %constant.114.clone.s_low) | copy-start | bytes 1572868
  36.0 46.3 %copy-start.3 = (bf16[512,512]{1,0:T(8,128)(2,1)S(1)}, bf16[512,512]{1,0:T(8,128)(2,1)}, u32[]{:S(2)}) copy-start(bf16[512,512]{1,0:T(8,128)(2,1)} %constant.113.clone.s_high) | copy-start | bytes 1572868
  36.1 46.3 %copy-start.14 = (f32[2,64,128]{2,1,0:T(8,128)S(1)}, f32[2,64,128]{2,1,0:T(8,128)}, u32[]{:S(2)}) copy-start(f32[2,64,128]{2,1,0:T(8,128)} %constant.117.clone.twiddle_ref) | copy-start | bytes 196612
  36.1 46.3 %copy-start.15 = (bf16[256,256]{1,0:T(8,128)(2,1)S(1)}, bf16[256,256]{1,0:T(8,128)(2,1)}, u32[]{:S(2)}) copy-start(bf16[256,256]{1,0:T(8,128)(2,1)} %constant.106.clone.a_low.refs_7_) | copy-start | bytes 393220
  36.1 46.3 %copy-start.16 = (bf16[256,256]{1,0:T(8,128)(2,1)S(1)}, bf16[256,256]{1,0:T(8,128)(2,1)}, u32[]{:S(2)}) copy-start(bf16[256,256]{1,0:T(8,128)(2,1)} %constant.105.clone.a_high.refs_6_) | copy-start | bytes 393220
  36.1 46.3 %copy-start.21 = (bf16[256,256]{1,0:T(8,128)(2,1)S(1)}, bf16[256,256]{1,0:T(8,128)(2,1)}, u32[]{:S(2)}) copy-start(bf16[256,256]{1,0:T(8,128)(2,1)} %constant.108.clone.b_low) | copy-start | bytes 393220
  36.1 46.3 %copy-start.25 = (bf16[256,256]{1,0:T(8,128)(2,1)S(1)}, bf16[256,256]{1,0:T(8,128)(2,1)}, u32[]{:S(2)}) copy-start(bf16[256,256]{1,0:T(8,128)(2,1)} %constant.107.clone.b_high) | copy-start | bytes 393220
  90.0 104.8 %all-to-all-start = ((f32[32,64,512]{2,1,0:T(8,128)}), f32[32,64,512]{2,1,0:T(8,128)}, u32[]{:S(2)}, u32[]{:S(2)}) async-start(f32[32,64,512]{2,1,0:T(8,128)} %cols_forward.4), calls=%async_computation | async-start | bytes 8388608 | tf_op jit(solution)/shard_map/all_to_all | solution.py:693
  109.5 78.6 %copy-start.17 = (bf16[256,256]{1,0:T(8,128)(2,1)S(1)}, bf16[256,256]{1,0:T(8,128)(2,1)}, u32[]{:S(2)}) copy-start(bf16[256,256]{1,0:T(8,128)(2,1)} %constant.105.clone.a_high.refs_6_) | copy-start | bytes 393220
  109.5 78.6 %copy-start.22 = (bf16[256,256]{1,0:T(8,128)(2,1)S(1)}, bf16[256,256]{1,0:T(8,128)(2,1)}, u32[]{:S(2)}) copy-start(bf16[256,256]{1,0:T(8,128)(2,1)} %constant.108.clone.b_low) | copy-start | bytes 393220
  109.5 78.6 %copy-start.26 = (bf16[256,256]{1,0:T(8,128)(2,1)S(1)}, bf16[256,256]{1,0:T(8,128)(2,1)}, u32[]{:S(2)}) copy-start(bf16[256,256]{1,0:T(8,128)(2,1)} %constant.107.clone.b_high) | copy-start | bytes 393220
  109.6 78.5 %collective-permute-start.3 = (f32[2,64,4096]{2,1,0:T(8,128)S(1)}, f32[2,64,4096]{2,1,0:T(8,128)S(1)}, u32[]{:S(2)}, u32[]{:S(2)}) collective-permute-start(f32[2,64,4096]{2,1,0:T(8,128)S(1)} %remap.11), channel_id=1, source_target_pairs={{0,1},{1,0},{2,3},{3,2},{4,5},{5,4},{6,7},{7,6},{8,9},{9,8},{10,11... | collective-permute-start | bytes 6291464 | tf_op jit(solution)/shard_map/ppermute | solution.py:690
  194.8 106.0 %all-to-all-start.1 = ((f32[32,64,512]{2,1,0:T(8,128)}), f32[32,64,512]{2,1,0:T(8,128)}, u32[]{:S(2)}, u32[]{:S(2)}) async-start(f32[32,64,512]{2,1,0:T(8,128)} %cols_forward.5), calls=%async_computation.1 | async-start | bytes 8388608 | tf_op jit(solution)/shard_map/all_to_all | solution.py:693
  215.5 78.6 %copy-start.18 = (bf16[256,256]{1,0:T(8,128)(2,1)S(1)}, bf16[256,256]{1,0:T(8,128)(2,1)}, u32[]{:S(2)}) copy-start(bf16[256,256]{1,0:T(8,128)(2,1)} %constant.105.clone.a_high.refs_6_) | copy-start | bytes 393220
  215.6 78.6 %copy-start.23 = (bf16[256,256]{1,0:T(8,128)(2,1)S(1)}, bf16[256,256]{1,0:T(8,128)(2,1)}, u32[]{:S(2)}) copy-start(bf16[256,256]{1,0:T(8,128)(2,1)} %constant.108.clone.b_low) | copy-start | bytes 393220
  215.6 78.6 %copy-start.27 = (bf16[256,256]{1,0:T(8,128)(2,1)S(1)}, bf16[256,256]{1,0:T(8,128)(2,1)}, u32[]{:S(2)}) copy-start(bf16[256,256]{1,0:T(8,128)(2,1)} %constant.107.clone.b_high) | copy-start | bytes 393220
  215.6 78.5 %collective-permute-start.4 = (f32[2,64,4096]{2,1,0:T(8,128)S(1)}, f32[2,64,4096]{2,1,0:T(8,128)S(1)}, u32[]{:S(2)}, u32[]{:S(2)}) collective-permute-start(f32[2,64,4096]{2,1,0:T(8,128)S(1)} %remap.13), channel_id=1, source_target_pairs={{0,1},{1,0},{2,3},{3,2},{4,5},{5,4},{6,7},{7,6},{8,9},{9,8},{10,11... | collective-permute-start | bytes 6291464 | tf_op jit(solution)/shard_map/ppermute | solution.py:690
  300.8 106.1 %all-to-all-start.2 = ((f32[32,64,512]{2,1,0:T(8,128)}), f32[32,64,512]{2,1,0:T(8,128)}, u32[]{:S(2)}, u32[]{:S(2)}) async-start(f32[32,64,512]{2,1,0:T(8,128)} %cols_forward.6), calls=%async_computation.2 | async-start | bytes 8388608 | tf_op jit(solution)/shard_map/all_to_all | solution.py:693
  321.6 78.6 %copy-start.19 = (bf16[256,256]{1,0:T(8,128)(2,1)S(1)}, bf16[256,256]{1,0:T(8,128)(2,1)}, u32[]{:S(2)}) copy-start(bf16[256,256]{1,0:T(8,128)(2,1)} %constant.105.clone.a_high.refs_6_) | copy-start | bytes 393220
  321.6 78.6 %copy-start.24 = (bf16[256,256]{1,0:T(8,128)(2,1)S(1)}, bf16[256,256]{1,0:T(8,128)(2,1)}, u32[]{:S(2)}) copy-start(bf16[256,256]{1,0:T(8,128)(2,1)} %constant.108.clone.b_low) | copy-start | bytes 393220
  321.6 78.6 %copy-start.28 = (bf16[256,256]{1,0:T(8,128)(2,1)S(1)}, bf16[256,256]{1,0:T(8,128)(2,1)}, u32[]{:S(2)}) copy-start(bf16[256,256]{1,0:T(8,128)(2,1)} %constant.107.clone.b_high) | copy-start | bytes 393220
  321.6 78.5 %collective-permute-start.5 = (f32[2,64,4096]{2,1,0:T(8,128)S(1)}, f32[2,64,4096]{2,1,0:T(8,128)S(1)}, u32[]{:S(2)}, u32[]{:S(2)}) collective-permute-start(f32[2,64,4096]{2,1,0:T(8,128)S(1)} %remap.15), channel_id=1, source_target_pairs={{0,1},{1,0},{2,3},{3,2},{4,5},{5,4},{6,7},{7,6},{8,9},{9,8},{10,11... | collective-permute-start | bytes 6291464 | tf_op jit(solution)/shard_map/ppermute | solution.py:690
  406.8 6.8 copy-start.37
  406.8 6.8 copy-start.38
  406.8 6.8 copy-start.1
  406.8 97.3 %all-to-all-start.3 = ((f32[32,64,512]{2,1,0:T(8,128)}), f32[32,64,512]{2,1,0:T(8,128)}, u32[]{:S(2)}, u32[]{:S(2)}) async-start(f32[32,64,512]{2,1,0:T(8,128)} %cols_forward.7), calls=%async_computation.3 | async-start | bytes 8388608 | tf_op jit(solution)/shard_map/all_to_all | solution.py:693
  504.2 6.6 copy-start.10
  504.2 6.6 copy-start.20
  504.2 6.6 copy-start.35
  504.2 6.6 copy-start.36
  541.5 54.8 %all-to-all-start.7 = ((f32[32,64,256]{2,1,0:T(8,128)}), f32[32,64,256]{2,1,0:T(8,128)S(1)}, u32[]{:S(2)}, u32[]{:S(2)}) async-start(f32[32,64,256]{2,1,0:T(8,128)} %bitcast.12), calls=%async_computation.7 | async-start | bytes 4194304 | tf_op jit(solution)/shard_map/all_to_all | solution.py:703
  597.6 52.4 %all-to-all-start.6 = ((f32[32,64,256]{2,1,0:T(8,128)}), f32[32,64,256]{2,1,0:T(8,128)S(1)}, u32[]{:S(2)}, u32[]{:S(2)}) async-start(f32[32,64,256]{2,1,0:T(8,128)} %bitcast.17), calls=%async_computation.6 | async-start | bytes 4194304 | tf_op jit(solution)/shard_map/all_to_all | solution.py:703
  650.0 10.4 %copy-start.4 = (f32[32,64,256]{2,1,0:T(8,128)}, f32[32,64,256]{2,1,0:T(8,128)S(1)}, u32[]{:S(2)}) copy-start(f32[32,64,256]{2,1,0:T(8,128)S(1)} %all-to-all-done.6.x_ref) | copy-start | bytes 6291460
  650.0 52.5 %all-to-all-start.5 = ((f32[32,64,256]{2,1,0:T(8,128)}), f32[32,64,256]{2,1,0:T(8,128)}, u32[]{:S(2)}, u32[]{:S(2)}) async-start(f32[32,64,256]{2,1,0:T(8,128)} %bitcast.16), calls=%async_computation.5 | async-start | bytes 4194304 | tf_op jit(solution)/shard_map/all_to_all | solution.py:703
  661.7 46.6 %copy-start.31 = (bf16[256,256]{1,0:T(8,128)(2,1)S(1)}, bf16[256,256]{1,0:T(8,128)(2,1)}, u32[]{:S(2)}) copy-start(bf16[256,256]{1,0:T(8,128)(2,1)} %constant.116.clone.s_low) | copy-start | bytes 393220
  661.7 46.6 %copy-start.32 = (bf16[256,256]{1,0:T(8,128)(2,1)S(1)}, bf16[256,256]{1,0:T(8,128)(2,1)}, u32[]{:S(2)}) copy-start(bf16[256,256]{1,0:T(8,128)(2,1)} %constant.115.clone.s_high) | copy-start | bytes 393220
  661.7 46.6 %copy-start.33 = (bf16[256,256]{1,0:T(8,128)(2,1)S(1)}, bf16[256,256]{1,0:T(8,128)(2,1)}, u32[]{:S(2)}) copy-start(bf16[256,256]{1,0:T(8,128)(2,1)} %constant.112.clone.g_low) | copy-start | bytes 393220
  661.8 46.7 %copy-start.34 = (bf16[256,256]{1,0:T(8,128)(2,1)S(1)}, bf16[256,256]{1,0:T(8,128)(2,1)}, u32[]{:S(2)}) copy-start(bf16[256,256]{1,0:T(8,128)(2,1)} %constant.111.clone.g_high) | copy-start | bytes 393220
  702.6 52.6 %all-to-all-start.4 = ((f32[32,64,256]{2,1,0:T(8,128)}), f32[32,64,256]{2,1,0:T(8,128)S(1)}, u32[]{:S(2)}, u32[]{:S(2)}) async-start(f32[32,64,256]{2,1,0:T(8,128)} %bitcast.15), calls=%async_computation.4 | async-start | bytes 4194304 | tf_op jit(solution)/shard_map/all_to_all | solution.py:703
  710.0 3.7 copy-start.5
  722.1 86.7 %collective-permute-start.7 = (f32[64,4096]{1,0:T(8,128)}, f32[64,4096]{1,0:T(8,128)}, u32[]{:S(2)}, u32[]{:S(2)}) collective-permute-start(f32[64,4096]{1,0:T(8,128)} %get-tuple-element.29), channel_id=1, source_target_pairs={{0,1},{1,0},{2,3},{3,2},{4,5},{5,4},{6,7},{7,6},{8,9},{9,8},{10,11... | collective-permute-start | bytes 3145736 | tf_op jit(solution)/shard_map/ppermute | solution.py:707
  723.6 83.2 %collective-permute-start.8 = (f32[64,4096]{1,0:T(8,128)}, f32[64,4096]{1,0:T(8,128)}, u32[]{:S(2)}, u32[]{:S(2)}) collective-permute-start(f32[64,4096]{1,0:T(8,128)} %get-tuple-element.30), channel_id=1, source_target_pairs={{0,1},{1,0},{2,3},{3,2},{4,5},{5,4},{6,7},{7,6},{8,9},{9,8},{10,11... | collective-permute-start | bytes 3145736 | tf_op jit(solution)/shard_map/ppermute | solution.py:707
  724.1 80.6 %collective-permute-start.9 = (f32[64,4096]{1,0:T(8,128)}, f32[64,4096]{1,0:T(8,128)}, u32[]{:S(2)}, u32[]{:S(2)}) collective-permute-start(f32[64,4096]{1,0:T(8,128)} %get-tuple-element.31), channel_id=1, source_target_pairs={{0,1},{1,0},{2,3},{3,2},{4,5},{5,4},{6,7},{7,6},{8,9},{9,8},{10,11... | collective-permute-start | bytes 3145736 | tf_op jit(solution)/shard_map/ppermute | solution.py:707
  758.6 68.1 %collective-permute-start.6 = (f32[64,4096]{1,0:T(8,128)S(1)}, f32[64,4096]{1,0:T(8,128)S(1)}, u32[]{:S(2)}, u32[]{:S(2)}) collective-permute-start(f32[64,4096]{1,0:T(8,128)S(1)} %get-tuple-element.28), channel_id=1, source_target_pairs={{0,1},{1,0},{2,3},{3,2},{4,5},{5,4},{6,7},{7,6},{8,9},{9,8},{10,11... | collective-permute-start | bytes 3145736 | tf_op jit(solution)/shard_map/ppermute | solution.py:707
  (9 other events, 15.1 us)

commit v2 on v1

--- a/solution.py
+++ b/solution.py
@@ -162,6 +162,51 @@
 def product(left, right):
     dot = lambda a, b: jnp.dot(a, b, preferred_element_type=jnp.float32)
     return dot(left[0], right[0]) + (dot(left[1], right[0]) + dot(left[0], right[1]))
+
+
+LOG_STEP = math.log(2.0) / 1024.0
+TOP = 32767.0
+
+
+def scale_code(largest):
+    return jnp.floor(jnp.log(jnp.maximum(largest, 1e-33)) / LOG_STEP).astype(jnp.int32) + 2
+
+
+def unit_of(code):
+    return jnp.exp(code.astype(jnp.float32) * LOG_STEP) * (1.0 / TOP)
+
+
+def pack(first, second, code):
+    inverse = 1.0 / unit_of(code)
+    a, b = (
+        jnp.clip(jnp.floor(x * inverse + 0.5), -TOP, TOP).astype(jnp.int32)
+        for x in (first, second)
+    )
+    return (a << 16) | (b & 0xFFFF)
+
+
+def unpack(packed, unit):
+    first, second = packed >> 16, (packed << 16) >> 16
+    return first.astype(jnp.float32) * unit, second.astype(jnp.float32) * unit
+
+
+def largest_of(first, second, axis):
+    return jnp.max(jnp.maximum(jnp.abs(first), jnp.abs(second)), axis=axis, keepdims=True)
+
+
+def put_row(ref, where, row, value):
+    old = ref[where]
+    lane_row = lax.broadcasted_iota(jnp.int32, old.shape, old.ndim - 2)
+    ref[where] = jnp.where(lane_row == row, value, jnp.where(row == 0, 0, old))
+
+
+def take_row(tile, row):
+    rows = lax.broadcasted_iota(jnp.int32, tile.shape, tile.ndim - 2)
+    return jnp.sum(jnp.where(rows == row, tile, 0), axis=tile.ndim - 2, keepdims=True)
+
+
+def scale_rows(count):
+    return -(-count // 8) * 8
 
 
 def halves(matrix):
@@ -233,24 +278,43 @@
 
 
 def remap_kernel(
-    half_ref, above_ref, below_ref, slopes_ref, source_ref, row_ref, pixel_ref, fraction_ref,
-    moves_ref, out_ref, window, picker, picked, moved,
+    coded, group, last, half_ref, above_ref, here_ref, below_ref, edge_ref, slopes_ref, source_ref,
+    row_ref, pixel_ref, fraction_ref, moves_ref, past_ref, out_ref, window, picker, picked, moved,
 ):
     tiles = slopes_ref.shape[2] // TILE
     span = 2 * GROUP
     count = PAIRS * tiles * GROUP
-    for t in range(tiles):
-        cols = slice(t * TILE, (t + 1) * TILE)
-        for p in range(2):
-            lanes = slice(p * TILE, (p + 1) * TILE)
-            window[t * span : t * span + GROUP, lanes] = above_ref[p, :, cols]
-            window[t * span + GROUP : (t + 1) * span, lanes] = below_ref[p, :, cols]
+    here = group(pl.program_id(0), pl.program_id(1), half_ref)
+    upper = lax.broadcasted_iota(jnp.int32, (GROUP, TILE), 0) < GROUP // 2
+
+    def fill(after_ref, before_ref):
+        for t in range(tiles):
+            cols = slice(t * TILE, (t + 1) * TILE)
+            for p in range(2):
+                lanes = slice(p * TILE, (p + 1) * TILE)
+                window[t * span : t * span + GROUP, lanes] = here_ref[p, :, cols]
+                window[t * span + GROUP : (t + 1) * span, lanes] = jnp.where(
+                    upper, after_ref[p, :, cols], before_ref[p, :, cols]
+                )
+
+    @pl.when((here > 0) & (here < last))
+    def _():
+        fill(below_ref, above_ref)
+
+    @pl.when(here == 0)
+    def _():
+        fill(below_ref, edge_ref)
+
+    @pl.when(here == last)
+    def _():
+        fill(edge_ref, above_ref)
+
     lane = lax.broadcasted_iota(jnp.int32, (GROUP, TILE), 1)
     down = lax.broadcasted_iota(jnp.int32, (GROUP, tiles), 0)
     per = TILE // span
     for k in range(PAIRS):
         source = source_ref[k]
-        place = (source % per) * span + down + HALO + row_ref[k]
+        place = (source % per) * span + ((down + row_ref[k]) & (span - 1))
         block = source // per
         for t in range(tiles):
             here = slice((k * tiles + t) * GROUP, (k * tiles + t + 1) * GROUP)
@@ -288,11 +352,22 @@
                 pulled[p] = term if pulled[p] is None else pulled[p] + term
         cols = slice(t * TILE, (t + 1) * TILE)
         slopes = [slopes_ref[i, :, cols].astype(jnp.float32) for i in range(4)]
-        out_ref[0, :, cols] = -(pulled[0] * slopes[0] + pulled[1] * slopes[1])
-        out_ref[1, :, cols] = -(pulled[0] * slopes[2] + pulled[1] * slopes[3])
-
-
-def remap_flow(half, part, parts, padded, slopes, source, row_shift, pixel_shift, fraction):
+        across = -(pulled[0] * slopes[0] + pulled[1] * slopes[1])
+        downward = -(pulled[0] * slopes[2] + pulled[1] * slopes[3])
+        if coded:
+            code = scale_code(largest_of(across, downward, 0))
+            step = pl.program_id(0) * pl.num_programs(1) + pl.program_id(1)
+            at = pl.ds(pl.multiple_of(step * GROUP, GROUP), GROUP)
+            out_ref[at, cols] = pack(across, downward, code)
+            put_row(out_ref, (slice(-8, None), cols), step, code)
+        else:
+            out_ref[0, :, cols] = across
+            out_ref[1, :, cols] = downward
+
+
+def remap_flow(
+    half, part, parts, coded, past, residual, edge, slopes, source, row_shift, pixel_shift, fraction
+):
     rows, cols = slopes.shape[1:]
     tiles = cols // TILE
     run = TILE // parts
@@ -302,27 +377,39 @@
     def group(l, i, half_ref):
         return half_ref[0] * half_groups + l * (TILE // GROUP) + part * steps + i
 
+    last = rows // GROUP - 1
     here = lambda l, i, half_ref: (0, group(l, i, half_ref), 0)
-    after = lambda l, i, half_ref: (0, group(l, i, half_ref) + 1, 0)
+    before = lambda l, i, half_ref: (0, jnp.maximum(group(l, i, half_ref) - 1, 0), 0)
+    after = lambda l, i, half_ref: (0, jnp.minimum(group(l, i, half_ref) + 1, last), 0)
     j = np.arange(TILE)
     moves = np.concatenate([j[:, None] == j[None, :] + step for step in STEPS], axis=1)
     small = pl.BlockSpec((PAIRS, GROUP, tiles), here)
     depth = 2 * GROUP * tiles
     count = PAIRS * GROUP * tiles
     runs = rows // 2 // TILE
+    if coded:
+        shape = (runs * run + scale_rows(runs * steps), cols)
+        out = jax.ShapeDtypeStruct(shape, jnp.int32)
+        out_spec = whole(shape)
+    else:
+        out = jax.ShapeDtypeStruct((2, runs * run, cols), jnp.float32)
+        out_spec = pl.BlockSpec((2, GROUP, cols), lambda l, i, _: (0, l * steps + i, 0))
     return pl.pallas_call(
-        remap_kernel,
+        partial(remap_kernel, coded, group, last),
         grid_spec=pltpu.PrefetchScalarGridSpec(
             num_scalar_prefetch=1,
             grid=(runs, steps),
             in_specs=[
+                pl.BlockSpec((2, GROUP, cols), before),
                 pl.BlockSpec((2, GROUP, cols), here),
                 pl.BlockSpec((2, GROUP, cols), after),
+                whole(edge.shape),
                 pl.BlockSpec((4, GROUP, cols), here),
                 small, small, small, small,
                 whole(moves.shape),
+                pl.BlockSpec(memory_space=pl.ANY),
             ],
-            out_specs=pl.BlockSpec((2, GROUP, cols), lambda l, i, _: (0, l * steps + i, 0)),
+            out_specs=out_spec,
             scratch_shapes=[
                 pltpu.VMEM((depth, 2 * TILE), jnp.bfloat16),
                 pltpu.VMEM((count, depth), jnp.bfloat16),
@@ -330,22 +417,23 @@
                 pltpu.VMEM((2 * count, len(STEPS) * TILE), jnp.float32),
             ],
         ),
-        out_shape=jax.ShapeDtypeStruct((2, runs * run, cols), jnp.float32),
+        out_shape=out,
         compiler_params=params(),
         cost_estimate=pl.CostEstimate(
-            flops=20_000_000 * runs * run, bytes_accessed=40 * runs * run * cols, transcendentals=0
+            flops=1000 if coded or part == 0 else 2 * 10**10, bytes_accessed=0, transcendentals=0
         ),
         name="remap",
-    )(half, padded, padded, slopes, source, row_shift, pixel_shift, fraction,
-      jnp.asarray(moves, jnp.bfloat16))
+    )(half, residual, residual, residual, edge, slopes, source, row_shift, pixel_shift, fraction,
+      jnp.asarray(moves, jnp.bfloat16), past)
 
 
 def cols_forward_kernel(
-    sign_ref, own_ref, got_ref, twiddle_ref, a_high, a_low, b_high, b_low, s_high, s_low,
+    sign_ref, own_ref, got_ref, code_ref, next_ref, twiddle_ref, a_high, a_low, b_high, b_low, s_high, s_low,
     out_ref, xa_high, xa_low, xb_high, xb_low, hold,
 ):
-    devices = out_ref.shape[0]
-    rows = out_ref.shape[1]
+    devices, rows, _ = xa_high.shape
+    total_rows = rows * pl.num_programs(0)
+    now = pl.program_id(0)
     sign = sign_ref[0]
 
     def block(r, carry):
@@ -365,7 +453,9 @@
 
         def both(t):
             cols = slice(t * TILE, (t + 1) * TILE)
-            return [(own_ref[p, at, cols], got_ref[p, at, cols]) for p in range(2)]
+            unit = unit_of(take_row(code_ref[:, cols], now * (rows // GROUP) + r))
+            got = unpack(got_ref[at, cols], unit)
+            return [(own_ref[p, at, cols], got[p]) for p in range(2)]
 
         def total(t):
             return tuple(a + b for a, b in both(t))
@@ -379,56 +469,77 @@
 
     lax.fori_loop(0, rows // GROUP, block, 0)
     flat = (devices - 1) * rows
+
+    def put_out(slots, which, re, im):
+        code = scale_code(largest_of(re, im, 1))
+        at = pl.ds(pl.multiple_of(which * total_rows + now * rows, GROUP), rows)
+        out_ref[slots, at, :] = pack(re, im, code)
+        put_row(out_ref, (slots, slice(-8, None)), 2 * now + which, code)
+
     for i, (high, low, mh, ml) in enumerate(
         ((xa_high, xa_low, a_high, a_low), (xb_high, xb_low, b_high, b_low))
     ):
         left = tuple(x[1:].reshape(flat, 2 * TILE) for x in (high, low))
-        value = product(left, (mh[...], ml[...]))
-        for part in range(2):
-            lanes = slice((2 * part + i) * TILE, (2 * part + i + 1) * TILE)
-            out_ref[1:, :, lanes] = value[:, part * TILE : (part + 1) * TILE].reshape(
-                devices - 1, rows, TILE
-            )
+        value = product(left, (mh[...], ml[...])).reshape(devices - 1, rows, 2 * TILE)
+        put_out(slice(1, devices), i, value[:, :, :TILE], value[:, :, TILE:])
     left = tuple(
         jnp.concatenate([xa[0], xb[0]], axis=1)
         for xa, xb in ((xa_high, xb_high), (xa_low, xb_low))
     )
-    out_ref[0] = product(left, (s_high[...], s_low[...]))
-
-
-def cols_forward(plan, sign, own, got):
+    value = product(left, (s_high[...], s_low[...])).reshape(1, rows, 4 * TILE)
+    for i in range(2):
+        put_out(
+            slice(0, 1), i, value[:, :, i * TILE : (i + 1) * TILE],
+            value[:, :, (i + 2) * TILE : (i + 3) * TILE],
+        )
+
+
+def cols_forward(plan, sign, own, got, later):
     rows, cols = own.shape[1:]
     d = plan.devices
     step = 2 * GROUP
     data = pl.BlockSpec((2, step, cols), lambda i: (0, i, 0))
+    codes = got.shape[0] - rows
+    shape = (d, 2 * rows + scale_rows(2 * rows // step), TILE)
     square = whole((2 * TILE, 2 * TILE))
     wide = whole((4 * TILE, 4 * TILE))
     return pl.pallas_call(
         cols_forward_kernel,
         grid=(rows // step,),
         in_specs=[
-            pl.BlockSpec(memory_space=pltpu.SMEM), data, data, whole(plan.col_twiddle.shape),
+            pl.BlockSpec(memory_space=pltpu.SMEM), data,
+            pl.BlockSpec((step, cols), lambda i: (i, 0)),
+            pl.BlockSpec((codes, cols), lambda i: (rows // codes, 0)),
+            pl.BlockSpec(memory_space=pl.ANY), whole(plan.col_twiddle.shape),
             square, square, square, square, wide, wide,
         ],
-        out_specs=pl.BlockSpec((d, step, 4 * TILE), lambda i: (0, i, 0)),
-        out_shape=jax.ShapeDtypeStruct((d, rows, 4 * TILE), jnp.float32),
+        out_specs=whole(shape),
+        out_shape=jax.ShapeDtypeStruct(shape, jnp.int32),
         scratch_shapes=[pltpu.VMEM((d, step, 2 * TILE), jnp.bfloat16)] * 4
         + [pltpu.VMEM((d, 2, GROUP, TILE), jnp.float32)],
         compiler_params=params(),
         cost_estimate=pl.CostEstimate(
-            flops=4096 * rows * cols, bytes_accessed=32 * rows * cols, transcendentals=0
+            flops=2 * 10**10, bytes_accessed=0, transcendentals=0
         ),
         name="cols_forward",
-    )(sign, own, got, plan.col_twiddle, *plan.list_a, *plan.list_b, *plan.special_forward)
-
-
-def rows_forward_kernel(x_ref, twiddle_ref, out_ref, hold):
-    tiles, _, lanes = x_ref.shape
+    )(sign, own, got, got, later, plan.col_twiddle, *plan.list_a, *plan.list_b, *plan.special_forward)
+
+
+def rows_forward_kernel(
+    run, a0_ref, a1_ref, b0_ref, b1_ref, code_ref, twiddle_ref, past_ref, out_ref, hold, unit
+):
+    tiles, step, lanes = out_ref.shape
     half = lanes // 2
     twiddle = (twiddle_ref[0], twiddle_ref[1])
+    unit[...] = unit_of(code_ref[...])
+    block = pl.program_id(0) * step // (2 * GROUP)
 
     def load(s):
-        return x_ref[s, :, :half], x_ref[s, :, half:]
+        g, l = s // 2, s % 2
+        at = 2 * (l * (run // (2 * GROUP)) + block)
+        a = unpack((a0_ref, a1_ref)[l][g], take_row(unit[g], at))
+        b = unpack((b0_ref, b1_ref)[l][g], take_row(unit[g], at + 1))
+        return tuple(jnp.concatenate(pair, axis=1) for pair in zip(a, b))
 
     def store(k, z):
         tc, ts = twiddle[0][:, k : k + 1], twiddle[1][:, k : k + 1]
@@ -438,25 +549,35 @@
     staged_dft(load, store, tiles, -1, hold)
 
 
-def rows_forward(plan, part, x):
-    tiles, rows, lanes = x.shape
+def rows_forward(plan, part, parts, x, past):
+    d = plan.devices
+    tiles = 2 * d
+    run = TILE // parts
+    lanes = 4 * TILE
     step = 8
+    codes = x.shape[1] - 4 * run
+    data = lambda k: pl.BlockSpec((d, step, TILE), lambda i: (0, k * (run // step) + i, 0))
     return pl.pallas_call(
-        rows_forward_kernel,
-        grid=(rows // step,),
-        in_specs=[
-            pl.BlockSpec((tiles, step, lanes), lambda i: (0, i, 0)),
-            pl.BlockSpec((2, step, tiles), lambda i: (0, part * (rows // step) + i, 0)),
+        partial(rows_forward_kernel, run),
+        grid=(run // step,),
+        in_specs=[data(k) for k in range(4)]
+        + [
+            pl.BlockSpec((d, codes, TILE), lambda i: (0, 4 * run // codes, 0)),
+            pl.BlockSpec((2, step, tiles), lambda i: (0, part * (run // step) + i, 0)),
+            pl.BlockSpec(memory_space=pl.ANY),
         ],
         out_specs=pl.BlockSpec((tiles, step, lanes), lambda i: (0, i, 0)),
-        out_shape=jax.ShapeDtypeStruct((tiles, rows, lanes), jnp.float32),
-        scratch_shapes=[pltpu.VMEM((tiles, 2, step, lanes // 2), jnp.float32)],
+        out_shape=jax.ShapeDtypeStruct((tiles, run, lanes), jnp.float32),
+        scratch_shapes=[
+            pltpu.VMEM((tiles, 2, step, lanes // 2), jnp.float32),
+            pltpu.VMEM((d, codes, TILE), jnp.float32),
+        ],
         compiler_params=params(),
         cost_estimate=pl.CostEstimate(
-            flops=64 * x.size, bytes_accessed=8 * x.size, transcendentals=0
+            flops=128 * x.size, bytes_accessed=12 * x.size, transcendentals=0
         ),
         name="rows_forward",
-    )(x, plan.row_twiddle)
+    )(x, x, x, x, x, plan.row_twiddle, past)
 
 
 def weigh_kernel(n, parts, *refs):
@@ -506,8 +627,9 @@
     )(*xs, *plan.rows_forward, *plan.rows_inverse, wave)
 
 
-def rows_inverse_kernel(x_ref, twiddle_ref, special_ref, out_ref, hold):
-    tiles, _, lanes = x_ref.shape
+def rows_inverse_kernel(run, x_ref, twiddle_ref, special_ref, past_ref, out_ref, hold, folded):
+    tiles, step, lanes = x_ref.shape
+    now = pl.program_id(0)
     half = lanes // 2
     twiddle = (twiddle_ref[0], twiddle_ref[1])
     special = special_ref[...] > 0.5
@@ -520,45 +642,66 @@
     def store(s, z):
         re_a, re_b = z[0][:, :TILE], z[0][:, TILE:]
         im_a, im_b = z[1][:, :TILE], z[1][:, TILE:]
-        out_ref[s, :, :TILE] = jnp.where(special, re_a, re_a + re_b)
-        out_ref[s, :, TILE:] = jnp.where(special, re_b, im_a - im_b)
+        folded[s, 0] = jnp.where(special, re_a, re_a + re_b)
+        folded[s, 1] = jnp.where(special, re_b, im_a - im_b)
 
     staged_dft(load, store, tiles, 1, hold)
-
-
-def rows_inverse(plan, part, parts, special, x):
+    for g in range(tiles // 2):
+        re, im = folded[2 * g : 2 * g + 2, 0], folded[2 * g : 2 * g + 2, 1]
+        code = scale_code(jnp.max(largest_of(re, im, 1), axis=0))
+        for l in range(2):
+            at = pl.ds(pl.multiple_of(l * run + now * step, 8), step)
+            out_ref[g, at, :] = pack(re[l], im[l], code)
+        put_row(out_ref, (g, slice(-8, None)), now, code)
+
+
+def rows_inverse(plan, part, parts, special, x, past):
     tiles, rows, lanes = x.shape
     step = 8
     run = rows // parts // step
+    shape = (tiles // 2, 2 * run * step + scale_rows(run), TILE)
     return pl.pallas_call(
-        rows_inverse_kernel,
+        partial(rows_inverse_kernel, run * step),
         grid=(run,),
         in_specs=[
             pl.BlockSpec((tiles, step, lanes), lambda i: (0, part * run + i, 0)),
             pl.BlockSpec((2, step, tiles), lambda i: (0, part * run + i, 0)),
             whole(special.shape),
+            pl.BlockSpec(memory_space=pl.ANY),
         ],
-        out_specs=pl.BlockSpec((tiles, step, lanes // 2), lambda i: (0, i, 0)),
-        out_shape=jax.ShapeDtypeStruct((tiles, rows // parts, lanes // 2), jnp.float32),
-        scratch_shapes=[pltpu.VMEM((tiles, 2, step, lanes // 2), jnp.float32)],
+        out_specs=whole(shape),
+        out_shape=jax.ShapeDtypeStruct(shape, jnp.int32),
+        scratch_shapes=[
+            pltpu.VMEM((tiles, 2, step, lanes // 2), jnp.float32),
+            pltpu.VMEM((tiles, 2, step, TILE), jnp.float32),
+        ],
         compiler_params=params(),
         cost_estimate=pl.CostEstimate(
             flops=64 * x.size // parts, bytes_accessed=6 * x.size // parts, transcendentals=0
         ),
         name="rows_inverse",
-    )(x, plan.row_twiddle, special)
+    )(x, plan.row_twiddle, special, past)
 
 
 def cols_inverse_kernel(
-    col_ref, sign_ref, x_ref, twiddle_ref, g_high, g_low, s_high, s_low, *rest,
+    col_ref, sign_ref, x_ref, code_ref, twiddle_ref, g_high, g_low, s_high, s_low, *rest,
 ):
     keep_ref, send_ref, spectrum, hold = rest[-4:]
     devices, rows, _ = x_ref.shape
     flat = (devices - 1) * rows
-    value = product(split(x_ref[1:].reshape(flat, 2 * TILE)), (g_high[...], g_low[...]))
+    per = pl.num_programs(1)
+    for j in range(rows // 8):
+        at = slice(8 * j, 8 * j + 8)
+        unit = unit_of(take_row(code_ref[...], pl.program_id(1) * (rows // 8) + j))
+        re, im = unpack(x_ref[:, at, :], unit)
+        spectrum[:, at, :TILE] = re
+        spectrum[:, at, TILE:] = im
+    value = product(split(spectrum[1:].reshape(flat, 2 * TILE)), (g_high[...], g_low[...]))
+    first = product(split(spectrum[0]), (s_high[...], s_low[...]))
     spectrum[1:] = value.reshape(devices - 1, rows, 2 * TILE)
-    spectrum[0] = product(split(x_ref[0]), (s_high[...], s_low[...]))
+    spectrum[0] = first
     sign = sign_ref[0]
+    step = pl.program_id(0) * per + pl.program_id(1)
 
     def block(r, carry):
         at = pl.ds(pl.multiple_of(r * GROUP, GROUP), GROUP)
@@ -579,11 +722,15 @@
             return a + c - odd[1], b - d + odd[0]
 
         def store(n, z):
-            for i in range(2):
-                t = 2 * n + i
-                ref = keep_ref if t < devices else send_ref
-                t %= devices
-                ref[at, t * TILE : (t + 1) * TILE] = z[i]
+            if 2 * n < devices:
+                for i in range(2):
+                    keep_ref[at, (2 * n + i) * TILE : (2 * n + i + 1) * TILE] = z[i]
+                return
+            cols = slice((n - devices // 2) * TILE, (n - devices // 2 + 1) * TILE)
+            code = scale_code(largest_of(z[0], z[1], 0))
+            down = pl.ds(pl.multiple_of(step * rows + r * GROUP, GROUP), GROUP)
+            send_ref[down, cols] = pack(z[0], z[1], code)
+            put_row(send_ref, (slice(-8, None), cols), step * (rows // GROUP) + r, code)
 
         staged_dft(load, store, devices, 1, hold)
         return carry
@@ -599,9 +746,12 @@
 
 
 def cols_inverse(plan, part, parts, half, sign, x, shape, image):
-    d, rows, _ = x.shape
+    d = plan.devices
     step = min(2 * GROUP, TILE // parts)
-    runs = rows * parts // TILE
+    runs = shape[0] // 2 // TILE
+    rows = runs * TILE // parts
+    codes = x.shape[1] - rows
+    sent = (rows + scale_rows(rows // GROUP), shape[1] // 2)
     per = TILE // parts // step
     cols = shape[1]
     square = whole((2 * TILE, 2 * TILE))
@@ -613,12 +763,13 @@
             num_scalar_prefetch=1,
             grid=(runs, per),
             in_specs=[
-                smem, pl.BlockSpec((d, step, 2 * TILE), lambda l, i, _: (0, l * per + i, 0)),
+                smem, pl.BlockSpec((d, step, TILE), lambda l, i, _: (0, l * per + i, 0)),
+                pl.BlockSpec((d, codes, TILE), lambda l, i, _: (0, rows // codes, 0)),
                 whole(plan.col_twiddle.shape), square, square, square, square,
             ] + [pl.BlockSpec(memory_space=pl.ANY)] * len(extra),
             out_specs=[
                 pl.BlockSpec((step, cols), place_block(part, parts, shape[0] // 2, step)),
-                pl.BlockSpec((step, cols), lambda l, i, _: (l * per + i, 0)),
+                whole(sent),
             ],
             scratch_shapes=[
                 pltpu.VMEM((d, step, 2 * TILE), jnp.float32),
@@ -627,25 +778,35 @@
         ),
         out_shape=[
             jax.ShapeDtypeStruct(shape, jnp.float32),
-            jax.ShapeDtypeStruct((rows, cols), jnp.float32),
+            jax.ShapeDtypeStruct(sent, jnp.int32),
         ],
-        input_output_aliases={8: 0} if extra else {},
+        input_output_aliases={9: 0} if extra else {},
         compiler_params=params(),
         cost_estimate=pl.CostEstimate(
             flops=2048 * x.size, bytes_accessed=8 * x.size, transcendentals=0
         ),
         name="cols_inverse",
-    )(half, sign, x, plan.col_twiddle, *plan.cols_inverse, *plan.special_inverse, *extra)
-
-
-def place_kernel(half_ref, got_ref, image_ref, out_ref):
-    out_ref[...] = got_ref[...]
+    )(half, sign, x, x, plan.col_twiddle, *plan.cols_inverse, *plan.special_inverse, *extra)
+
+
+def place_kernel(half_ref, got_ref, code_ref, image_ref, out_ref):
+    rows, cols = got_ref.shape
+    step = pl.program_id(0) * pl.num_programs(1) + pl.program_id(1)
+    for r in range(rows // GROUP):
+        at = slice(r * GROUP, (r + 1) * GROUP)
+        for n in range(cols // TILE):
+            lanes = slice(n * TILE, (n + 1) * TILE)
+            unit = unit_of(take_row(code_ref[:, lanes], step * (rows // GROUP) + r))
+            for i, value in enumerate(unpack(got_ref[at, lanes], unit)):
+                out_ref[at, (2 * n + i) * TILE : (2 * n + i + 1) * TILE] = value
 
 
 def place_rows(part, parts, half, got, image):
-    rows, cols = got.shape
+    cols = image.shape[1]
     step = min(2 * GROUP, TILE // parts)
-    runs = rows * parts // TILE
+    runs = image.shape[0] // 2 // TILE
+    rows = runs * TILE // parts
+    codes = got.shape[0] - rows
     per = TILE // parts // step
     return pl.pallas_call(
         place_kernel,
@@ -653,7 +814,8 @@
             num_scalar_prefetch=1,
             grid=(runs, per),
             in_specs=[
-                pl.BlockSpec((step, cols), lambda l, i, _: (l * per + i, 0)),
+                pl.BlockSpec((step, cols // 2), lambda l, i, _: (l * per + i, 0)),
+                pl.BlockSpec((codes, cols // 2), lambda l, i, _: (rows // codes, 0)),
                 pl.BlockSpec(memory_space=pl.ANY),
             ],
             out_specs=pl.BlockSpec(
@@ -661,11 +823,11 @@
             ),
         ),
         out_shape=jax.ShapeDtypeStruct(image.shape, jnp.float32),
-        input_output_aliases={2: 0},
+        input_output_aliases={3: 0},
         compiler_params=params(),
         cost_estimate=pl.CostEstimate(flops=0, bytes_accessed=8 * got.size, transcendentals=0),
         name="place_rows",
-    )(half, got, image)
+    )(half, got, got, image)
 
 
 def paired(residual, field_slopes, source_tile, row_shift, pixel_shift, fraction):
@@ -679,33 +841,52 @@
     sign = (1 - 2 * col).astype(jnp.float32).reshape(1)
     swap = [(0, 1), (1, 0)]
     both = ("rows", "cols")
-    padded = with_halo(residual, (("rows", 1),), HALO)
-    args = (padded, field_slopes, source_tile, row_shift, pixel_shift, fraction)
+    before = lax.ppermute(
+        residual[:, rows_dev - HALO :], "rows", [(k, k + 1) for k in range(devices // 2 - 1)]
+    )
+    after = lax.ppermute(
+        residual[:, :HALO], "rows", [(k + 1, k) for k in range(devices // 2 - 1)]
+    )
+    edge = jnp.concatenate([after, before], axis=1)
+    args = (residual, edge, field_slopes, source_tile, row_shift, pixel_shift, fraction)
     lane = jnp.arange(TILE, dtype=jnp.int32).reshape(1, TILE)
     special = jnp.where((lane == 0) & (place == 0), 1.0, 0.0)
     wave = plan.wave_of_lists(place)
     spectra = []
+    spectra, lists, aways, gots = [], [], [], []
+
+    def send(m, past):
+        aways.append(remap_flow(other, m, parts, True, past, *args))
+        gots.append(lax.ppermute(aways[m], "cols", swap))
+
+    send(0, special)
+    if parts > 1:
+        send(1, aways[0])
     for m in range(parts):
-        away = remap_flow(other, m, parts, *args)
-        got = lax.ppermute(away, "cols", swap)
-        own = remap_flow(mine, m, parts, *args)
-        lists = cols_forward(plan, sign, own, got)
-        lists = lax.all_to_all(lists, both, split_axis=0, concat_axis=0, tiled=True)
-        rows = lists.shape[1]
-        lists = lists.reshape(2 * devices, rows // 2, 4 * TILE)
-        spectra.append(rows_forward(plan, m, lists))
+        past = gots[m] if m or parts == 1 else aways[1]
+        own = remap_flow(mine, m, parts, False, past, *args)
+        past = spectra[m - 2] if m > 1 else special
+        lists.append(cols_forward(plan, sign, own, gots[m], past))
+        if m + 2 < parts:
+            send(m + 2, lists[m])
+        swapped = lax.all_to_all(lists[m], both, split_axis=0, concat_axis=0, tiled=True)
+        past = spectra[m - 1] if m else special
+        spectra.append(rows_forward(plan, m, parts, swapped, past))
     mixed = weigh(plan, wave, spectra)
     image = None
     sent = []
+    past = [special, special]
     for m in range(parts):
-        folded = rows_inverse(plan, m, parts, special, mixed)
-        folded = folded.reshape(devices, 2 * folded.shape[1], 2 * TILE)
+        folded = rows_inverse(plan, m, parts, special, mixed, past[m])
         folded = lax.all_to_all(folded, both, split_axis=0, concat_axis=0, tiled=True)
+        if m > 1:
+            image = place_rows(m - 2, parts, other, sent[m - 2], image)
         image, away = cols_inverse(
             plan, m, parts, mine, sign, folded, (rows_dev, cols_dev), image
         )
+        past.append(away)
         sent.append(lax.ppermute(away, "cols", swap))
-    for m in range(parts):
+    for m in range(max(parts - 2, 0), parts):
         image = place_rows(m, parts, other, sent[m], image)
     return image
 

time: 836 us -> 515 us (0.62)
  the two profiles are of different devices: /device:TPU:12 before, /device:TPU:0 now
where the time goes in v2:
time: 515 us; the launch traced here: 505 us
  Pallas kernels  248 us (48%)
  waiting for transfers between devices  181 us (35%)
  starting transfers between devices  47.8 us (9%)
  local copies, waits for them, and re-layouts  26.5 us (5%)
    pallas_call x8, Pallas kernels, remap_flow(): pl.pallas_call(partial(remap_kernel, coded, group, last), grid_spec=pltpu...  122 us
    all_to_all x4, waiting for transfers between devices, paired(): lax.all_to_all(lists[m], both, split_axis=0, concat_axis=0, tiled=True)  71.4 us
    all_to_all x4, waiting for transfers between devices, paired(): lax.all_to_all(folded, both, split_axis=0, concat_axis=0, tiled=True)  58.2 us
    ppermute x4, waiting for transfers between devices, paired(): sent.append(lax.ppermute(away, 'cols', swap))  51.8 us
    pallas_call x4, Pallas kernels, cols_forward(): pl.pallas_call(cols_forward_kernel, grid=(rows // step,), in_specs=[pl.Bl...  37.6 us
    unnamed x135, local copies, waits for them, and re-layouts  25.5 us
    pallas_call x1, Pallas kernels, weigh(): pl.pallas_call(partial(weigh_kernel, plan.n, parts), grid=(tiles // batch...  25.4 us
    pallas_call x4, Pallas kernels, rows_inverse(): pl.pallas_call(partial(rows_inverse_kernel, run * step), grid=(run,), in_...  21.8 us
  transfers between devices with their start and end apart: 18, of which 10 were waited for; matrix products, arithmetic and copies ran while one was open for 1% of the time, Pallas kernels for 38%

profile of v2, /device:TPU:0, one launch (start us, length us, event | category | flops | bytes accessed | tf_op | source)
XLA Modules:
  0.0 505.1 jit_solution(15636287728741835301)
XLA Ops:
  2.3 3.0 collective-permute-start.1
  9.0 16.2 %remap.8.past_ref = s32[72,4096]{1,0:T(8,128)} custom-call(s32[1]{0:T(128)} %bitcast.half_ref, bf16[2,512,4096]{2,1,0:T(8,128)(2,1)} %below_ref.15, bf16[2,512,4096]{2,1,0:T(8,128)(2,1)} %below_ref.15, bf16[2,512,4096]{2,1,0:T(8,128)(2,1)} %below_ref.15, bf16[2,16,4096]{2,1,0:T(8,128)(2,1)S(1)} %constant_dynamic-update-slice_fusion.edge_ref, ...), custom_call_target="tpu_custom_call" | custom-call | flops 1000 | tf_op jit(solution)/shard_map/remap/pallas_call | solution.py:397
  25.3 2.9 collective-permute-start.2
  28.2 16.1 %remap.9.past_ref = s32[72,4096]{1,0:T(8,128)} custom-call(s32[1]{0:T(128)} %bitcast.half_ref, bf16[2,512,4096]{2,1,0:T(8,128)(2,1)} %below_ref.15, bf16[2,512,4096]{2,1,0:T(8,128)(2,1)} %below_ref.15, bf16[2,512,4096]{2,1,0:T(8,128)(2,1)} %below_ref.15, bf16[2,16,4096]{2,1,0:T(8,128)(2,1)S(1)} %constant_dynamic-update-slice_fusion.edge_ref, ...), custom_call_target="tpu_custom_call" | custom-call | flops 1000 | tf_op jit(solution)/shard_map/remap/pallas_call | solution.py:397
  44.4 14.4 %remap.10.own_ref = f32[2,64,4096]{2,1,0:T(8,128)S(1)} custom-call(s32[1]{0:T(128)} %bitcast.1.half_ref.col_ref, bf16[2,512,4096]{2,1,0:T(8,128)(2,1)} %below_ref.15, bf16[2,512,4096]{2,1,0:T(8,128)(2,1)} %below_ref.15, bf16[2,512,4096]{2,1,0:T(8,128)(2,1)} %below_ref.15, bf16[2,16,4096]{2,1,0:T(8,128)(2,1)S(1)} %constant_dynamic-update-slice_fusion.edge_ref, ...), custom_call_target="tpu_custom_call" | custom-call | flops 1000 | tf_op jit(solution)/shard_map/remap/pallas_call | solution.py:397
  58.9 9.7 %cols_forward.4.past_ref = s32[32,136,128]{2,1,0:T(8,128)} custom-call(f32[1]{0:T(128)} %bitcast.2.sign_ref, f32[2,64,4096]{2,1,0:T(8,128)S(1)} %remap.10.own_ref, s32[72,4096]{1,0:T(8,128)} %collective-permute-done.2.got_ref.code_ref, s32[72,4096]{1,0:T(8,128)} %collective-permute-done.2.got_ref.code_ref, ...), custom_call_target="tpu_custom_call" | custom-call | flops 20000000000 | tf_op jit(solution)/shard_map/cols_forward/pallas_call | solution.py:506
  68.7 7.3 %all-to-all-start = ((s32[32,136,128]{2,1,0:T(8,128)}), s32[32,136,128]{2,1,0:T(8,128)S(1)}, u32[]{:S(2)}, u32[]{:S(2)}) async-start(s32[32,136,128]{2,1,0:T(8,128)} %cols_forward.4.past_ref), calls=%async_computation | async-start | bytes 4456448 | tf_op jit(solution)/shard_map/all_to_all | solution.py:872
  80.6 16.1 %remap.12 = s32[72,4096]{1,0:T(8,128)} custom-call(s32[1]{0:T(128)} %bitcast.half_ref, bf16[2,512,4096]{2,1,0:T(8,128)(2,1)} %below_ref.15, bf16[2,512,4096]{2,1,0:T(8,128)(2,1)} %below_ref.15, bf16[2,512,4096]{2,1,0:T(8,128)(2,1)} %below_ref.15, bf16[2,16,4096]{2,1,0:T(8,128)(2,1)S(1)} %constant_dynamic-update-slice_fusion.edge_ref, ...), custom_call_target="tpu_custom_call" | custom-call | flops 1000 | tf_op jit(solution)/shard_map/remap/pallas_call | solution.py:397
  96.7 1.8 collective-permute-start.4
  98.5 14.2 %remap.11.own_ref = f32[2,64,4096]{2,1,0:T(8,128)S(1)} custom-call(s32[1]{0:T(128)} %bitcast.1.half_ref.col_ref, bf16[2,512,4096]{2,1,0:T(8,128)(2,1)} %below_ref.15, bf16[2,512,4096]{2,1,0:T(8,128)(2,1)} %below_ref.15, bf16[2,512,4096]{2,1,0:T(8,128)(2,1)} %below_ref.15, bf16[2,16,4096]{2,1,0:T(8,128)(2,1)S(1)} %constant_dynamic-update-slice_fusion.edge_ref, ...), custom_call_target="tpu_custom_call" | custom-call | flops 20000000000 | tf_op jit(solution)/shard_map/remap/pallas_call | solution.py:397
  112.8 9.3 %cols_forward.5.past_ref = s32[32,136,128]{2,1,0:T(8,128)} custom-call(f32[1]{0:T(128)} %bitcast.2.sign_ref, f32[2,64,4096]{2,1,0:T(8,128)S(1)} %remap.11.own_ref, s32[72,4096]{1,0:T(8,128)} %collective-permute-done.3.past_ref.got_ref.code_ref, s32[72,4096]{1,0:T(8,128)} %collective-permute-done.3.past_ref.got_ref.code_ref, ...), custom_call_target="tpu_custom_call" | custom-call | flops 20000000000 | tf_op jit(solution)/shard_map/cols_forward/pallas_call | solution.py:506
  122.1 5.4 %all-to-all-done.a0_ref.a1_ref.b0_ref.b1_ref.code_ref = s32[32,136,128]{2,1,0:T(8,128)S(1)} async-done(((s32[32,136,128]{2,1,0:T(8,128)}), s32[32,136,128]{2,1,0:T(8,128)S(1)}, u32[]{:S(2)}, u32[]{:S(2)}) %all-to-all-start) | async-done | bytes 2228256 | tf_op jit(solution)/shard_map/all_to_all | solution.py:872
  128.9 3.8 all-to-all-start.1
  137.4 16.2 %remap.14 = s32[72,4096]{1,0:T(8,128)} custom-call(s32[1]{0:T(128)} %bitcast.half_ref, bf16[2,512,4096]{2,1,0:T(8,128)(2,1)} %below_ref.15, bf16[2,512,4096]{2,1,0:T(8,128)(2,1)} %below_ref.15, bf16[2,512,4096]{2,1,0:T(8,128)(2,1)} %below_ref.15, bf16[2,16,4096]{2,1,0:T(8,128)(2,1)S(1)} %constant_dynamic-update-slice_fusion.edge_ref, ...), custom_call_target="tpu_custom_call" | custom-call | flops 1000 | tf_op jit(solution)/shard_map/remap/pallas_call | solution.py:397
  153.6 1.9 collective-permute-start.5
  156.4 14.2 %remap.13.own_ref = f32[2,64,4096]{2,1,0:T(8,128)S(1)} custom-call(s32[1]{0:T(128)} %bitcast.1.half_ref.col_ref, bf16[2,512,4096]{2,1,0:T(8,128)(2,1)} %below_ref.15, bf16[2,512,4096]{2,1,0:T(8,128)(2,1)} %below_ref.15, bf16[2,512,4096]{2,1,0:T(8,128)(2,1)} %below_ref.15, bf16[2,16,4096]{2,1,0:T(8,128)(2,1)S(1)} %copy-done.17, ...), custom_call_target="tpu_custom_call" | custom-call | flops 20000000000 | tf_op jit(solution)/shard_map/remap/pallas_call | solution.py:397
  170.8 4.4 rows_forward.4.past_ref.next_ref.refs_0_
  175.3 9.3 %cols_forward.6 = s32[32,136,128]{2,1,0:T(8,128)} custom-call(f32[1]{0:T(128)} %bitcast.2.sign_ref, f32[2,64,4096]{2,1,0:T(8,128)S(1)} %remap.13.own_ref, s32[72,4096]{1,0:T(8,128)} %collective-permute-done.4.past_ref.got_ref.code_ref, s32[72,4096]{1,0:T(8,128)} %collective-permute-done.4.past_ref.got_ref.code_ref, ...), custom_call_target="tpu_custom_call" | custom-call | flops 20000000000 | tf_op jit(solution)/shard_map/cols_forward/pallas_call | solution.py:506
  185.9 5.0 all-to-all-start.2
  195.0 14.2 %remap.15.own_ref = f32[2,64,4096]{2,1,0:T(8,128)S(1)} custom-call(s32[1]{0:T(128)} %bitcast.1.half_ref.col_ref, bf16[2,512,4096]{2,1,0:T(8,128)(2,1)} %below_ref.15, bf16[2,512,4096]{2,1,0:T(8,128)(2,1)} %below_ref.15, bf16[2,512,4096]{2,1,0:T(8,128)(2,1)} %below_ref.15, bf16[2,16,4096]{2,1,0:T(8,128)(2,1)S(1)} %copy-done.18, ...), custom_call_target="tpu_custom_call" | custom-call | flops 20000000000 | tf_op jit(solution)/shard_map/remap/pallas_call | solution.py:397
  209.3 4.6 rows_forward.5.past_ref.next_ref.refs_1_
  214.0 9.3 %cols_forward.7 = s32[32,136,128]{2,1,0:T(8,128)} custom-call(f32[1]{0:T(128)} %bitcast.2.sign_ref, f32[2,64,4096]{2,1,0:T(8,128)S(1)} %remap.15.own_ref, s32[72,4096]{1,0:T(8,128)} %collective-permute-done.5.past_ref.got_ref.code_ref, s32[72,4096]{1,0:T(8,128)} %collective-permute-done.5.past_ref.got_ref.code_ref, ...), custom_call_target="tpu_custom_call" | custom-call | flops 20000000000 | tf_op jit(solution)/shard_map/cols_forward/pallas_call | solution.py:506
  223.3 19.1 %all-to-all-done.2.a0_ref.a1_ref.b0_ref.b1_ref.code_ref = s32[32,136,128]{2,1,0:T(8,128)S(1)} async-done(((s32[32,136,128]{2,1,0:T(8,128)}), s32[32,136,128]{2,1,0:T(8,128)S(1)}, u32[]{:S(2)}, u32[]{:S(2)}) %all-to-all-start.2) | async-done | bytes 2228256 | tf_op jit(solution)/shard_map/all_to_all | solution.py:872
  242.4 3.8 all-to-all-start.3
  246.3 4.7 rows_forward.6.past_ref.refs_2_
  250.9 46.8 %all-to-all-done.3.a0_ref.a1_ref.b0_ref.b1_ref.code_ref = s32[32,136,128]{2,1,0:T(8,128)} async-done(((s32[32,136,128]{2,1,0:T(8,128)}), s32[32,136,128]{2,1,0:T(8,128)}, u32[]{:S(2)}, u32[]{:S(2)}) %all-to-all-start.3) | async-done | bytes 2228256 | tf_op jit(solution)/shard_map/all_to_all | solution.py:872
  297.8 6.2 %rows_forward.7.refs_3_ = f32[64,32,512]{2,1,0:T(8,128)} custom-call(s32[32,136,128]{2,1,0:T(8,128)} %all-to-all-done.3.a0_ref.a1_ref.b0_ref.b1_ref.code_ref, s32[32,136,128]{2,1,0:T(8,128)} %all-to-all-done.3.a0_ref.a1_ref.b0_ref.b1_ref.code_ref, s32[32,136,128]{2,1,0:T(8,128)} %all-to-all-done.3.a0_ref.a1_ref.b0_ref.b1_ref.code_ref, ...), custom_call_target="tpu_custom_call" | custom-call | flops 71303168 | bytes 6684672 | tf_op jit(solution)/shard_map/rows_forward/pallas_call | solution.py:560
  304.0 25.4 %weigh.1.x_ref = f32[64,128,512]{2,1,0:T(8,128)} custom-call(f32[64,32,512]{2,1,0:T(8,128)S(1)} %copy-done.12, f32[64,32,512]{2,1,0:T(8,128)} %rows_forward.5.past_ref.next_ref.refs_1_, f32[64,32,512]{2,1,0:T(8,128)} %rows_forward.6.past_ref.refs_2_, f32[64,32,512]{2,1,0:T(8,128)} %rows_forward.7.refs_3_, bf16[256,256]{1,0:T(8,128)(2,1)S(1)} %copy-done.53, ...), custom_call_target="tpu_custom_call" | custom-call | flops 17179869184 | bytes 33554432 | tf_op jit(solution)/shard_map/weigh/pallas_call | solution.py:615
  329.4 6.2 %rows_inverse.5 = s32[32,72,128]{2,1,0:T(8,128)} custom-call(f32[64,128,512]{2,1,0:T(8,128)} %weigh.1.x_ref, f32[2,128,64]{2,1,0:T(8,128)S(1)} %copy-done.15, f32[1,128]{1,0:T(1,128)S(1)} %and_select_fusion.1.past_ref.next_ref.special_ref, f32[1,128]{1,0:T(1,128)S(1)} %and_select_fusion.1.past_ref.next_ref.special_ref), custom_call_target="tpu_custom_call" | custom-call | flops 67108864 | bytes 6291456 | tf_op jit(solution)/shard_map/rows_inverse/pallas_call | solution.py:663
  335.6 3.7 all-to-all-start.5
  339.2 5.2 %rows_inverse.4 = s32[32,72,128]{2,1,0:T(8,128)S(1)} custom-call(f32[64,128,512]{2,1,0:T(8,128)} %weigh.1.x_ref, f32[2,128,64]{2,1,0:T(8,128)S(1)} %copy-done.15, f32[1,128]{1,0:T(1,128)S(1)} %and_select_fusion.1.past_ref.next_ref.special_ref, f32[1,128]{1,0:T(1,128)S(1)} %and_select_fusion.1.past_ref.next_ref.special_ref), custom_call_target="tpu_custom_call" | custom-call | flops 67108864 | bytes 6291456 | tf_op jit(solution)/shard_map/rows_inverse/pallas_call | solution.py:663
  345.5 22.8 %all-to-all-done.5.x_ref.code_ref = s32[32,72,128]{2,1,0:T(8,128)S(1)} async-done(((s32[32,72,128]{2,1,0:T(8,128)}), s32[32,72,128]{2,1,0:T(8,128)S(1)}, u32[]{:S(2)}, u32[]{:S(2)}) %all-to-all-start.5) | async-done | bytes 1179680 | tf_op jit(solution)/shard_map/all_to_all | solution.py:881
  368.3 3.9 all-to-all-start.4
  372.2 4.3 cols_inverse.4
  376.5 5.2 %rows_inverse.7 = s32[32,72,128]{2,1,0:T(8,128)S(1)} custom-call(f32[64,128,512]{2,1,0:T(8,128)} %weigh.1.x_ref, f32[2,128,64]{2,1,0:T(8,128)S(1)} %copy-done.15, f32[1,128]{1,0:T(1,128)S(1)} %and_select_fusion.1.past_ref.next_ref.special_ref, s32[72,2048]{1,0:T(8,128)S(1)} %get-tuple-element.27.past_ref), custom_call_target="tpu_custom_call" | custom-call | flops 67108864 | bytes 6291456 | tf_op jit(solution)/shard_map/rows_inverse/pallas_call | solution.py:663
  383.5 17.7 %all-to-all-done.4.x_ref.code_ref = s32[32,72,128]{2,1,0:T(8,128)S(1)} async-done(((s32[32,72,128]{2,1,0:T(8,128)}), s32[32,72,128]{2,1,0:T(8,128)S(1)}, u32[]{:S(2)}, u32[]{:S(2)}) %all-to-all-start.4) | async-done | bytes 1179680 | tf_op jit(solution)/shard_map/all_to_all | solution.py:881
  401.2 3.6 all-to-all-start.7
  404.8 4.3 cols_inverse.5
  409.1 5.2 %rows_inverse.6 = s32[32,72,128]{2,1,0:T(8,128)S(1)} custom-call(f32[64,128,512]{2,1,0:T(8,128)} %weigh.1.x_ref, f32[2,128,64]{2,1,0:T(8,128)S(1)} %copy-done.15, f32[1,128]{1,0:T(1,128)S(1)} %and_select_fusion.1.past_ref.next_ref.special_ref, s32[72,2048]{1,0:T(8,128)S(1)} %get-tuple-element.26.past_ref), custom_call_target="tpu_custom_call" | custom-call | flops 67108864 | bytes 6291456 | tf_op jit(solution)/shard_map/rows_inverse/pallas_call | solution.py:663
  416.2 17.7 %all-to-all-done.7.x_ref.code_ref = s32[32,72,128]{2,1,0:T(8,128)S(1)} async-done(((s32[32,72,128]{2,1,0:T(8,128)}), s32[32,72,128]{2,1,0:T(8,128)S(1)}, u32[]{:S(2)}, u32[]{:S(2)}) %all-to-all-start.7) | async-done | bytes 1179680 | tf_op jit(solution)/shard_map/all_to_all | solution.py:881
  433.9 3.6 all-to-all-start.6
  437.5 1.8 collective-permute-start.7
  439.6 26.1 %collective-permute-done.7.got_ref.code_ref = s32[72,2048]{1,0:T(8,128)S(1)} collective-permute-done((s32[72,2048]{1,0:T(8,128)}, s32[72,2048]{1,0:T(8,128)S(1)}, u32[]{:S(2)}, u32[]{:S(2)}) %collective-permute-start.7) | collective-permute-done | bytes 589856 | tf_op jit(solution)/shard_map/ppermute | solution.py:888
  466.8 4.5 cols_inverse.6
  471.3 7.5 %collective-permute-done.6.got_ref.code_ref = s32[72,2048]{1,0:T(8,128)S(1)} collective-permute-done((s32[72,2048]{1,0:T(8,128)}, s32[72,2048]{1,0:T(8,128)S(1)}, u32[]{:S(2)}, u32[]{:S(2)}) %collective-permute-start.6) | collective-permute-done | bytes 589856 | tf_op jit(solution)/shard_map/ppermute | solution.py:888
  479.8 4.3 cols_inverse.7
  484.2 7.2 %collective-permute-done.9.got_ref.code_ref = s32[72,2048]{1,0:T(8,128)S(1)} collective-permute-done((s32[72,2048]{1,0:T(8,128)}, s32[72,2048]{1,0:T(8,128)S(1)}, u32[]{:S(2)}, u32[]{:S(2)}) %collective-permute-start.9) | collective-permute-done | bytes 589856 | tf_op jit(solution)/shard_map/ppermute | solution.py:888
  492.5 11.1 %collective-permute-done.8.got_ref.code_ref = s32[72,2048]{1,0:T(8,128)S(1)} collective-permute-done((s32[72,2048]{1,0:T(8,128)S(1)}, s32[72,2048]{1,0:T(8,128)S(1)}, u32[]{:S(2)}, u32[]{:S(2)}) %collective-permute-start.8) | collective-permute-done | bytes 589856 | tf_op jit(solution)/shard_map/ppermute | solution.py:888
  (157 shorter events, 32.7 us)
Async XLA Ops:
  0.0 9.0 %copy-start.19 = (bf16[128,768]{1,0:T(8,128)(2,1)S(1)}, bf16[128,768]{1,0:T(8,128)(2,1)}, u32[]{:S(2)}) copy-start(bf16[128,768]{1,0:T(8,128)(2,1)} %constant.120.clone.moves_ref) | copy-start | bytes 589828
  1.0 7.9 %collective-permute-start = (bf16[2,8,4096]{2,1,0:T(8,128)(2,1)S(1)}, bf16[2,8,4096]{2,1,0:T(8,128)(2,1)S(1)}, u32[]{:S(2)}, u32[]{:S(2)}) collective-permute-start(bf16[2,8,4096]{2,1,0:T(8,128)(2,1)S(1)} %get-tuple-element.34), channel_id=1, source_target_pairs={{2,0},{4,2},{6,4},{8,6},{10,8},{12,10},{14,12},{16,14},{18,16},{20... | collective-permute-start | bytes 393224 | tf_op jit(solution)/shard_map/ppermute | solution.py:847
  2.3 6.7 %collective-permute-start.1 = (bf16[2,8,4096]{2,1,0:T(8,128)(2,1)S(1)}, bf16[2,8,4096]{2,1,0:T(8,128)(2,1)S(1)}, u32[]{:S(2)}, u32[]{:S(2)}) collective-permute-start(bf16[2,8,4096]{2,1,0:T(8,128)(2,1)S(1)} %get-tuple-element.33), channel_id=1, source_target_pairs={{0,2},{2,4},{4,6},{6,8},{8,10},{10,12},{12,14},{14,16},{16,18},{18... | collective-permute-start | bytes 393224 | tf_op jit(solution)/shard_map/ppermute | solution.py:844
  8.7 35.6 %copy-start.4 = (s32[2,512,32]{2,1,0:T(8,128)}, s32[2,512,32]{2,1,0:T(8,128)S(1)}, u32[]{:S(2)}) copy-start(s32[2,512,32]{2,1,0:T(8,128)S(1)} %copy.49.pixel_ref) | copy-start | bytes 393220
  8.9 35.4 %copy-start.8 = (f32[2,512,32]{2,1,0:T(8,128)}, f32[2,512,32]{2,1,0:T(8,128)S(1)}, u32[]{:S(2)}) copy-start(f32[2,512,32]{2,1,0:T(8,128)S(1)} %copy.50.fraction_ref) | copy-start | bytes 393220
  9.0 123.7 %copy-start.16 = (bf16[2,16,4096]{2,1,0:T(8,128)(2,1)}, bf16[2,16,4096]{2,1,0:T(8,128)(2,1)S(1)}, u32[]{:S(2)}) copy-start(bf16[2,16,4096]{2,1,0:T(8,128)(2,1)S(1)} %constant_dynamic-update-slice_fusion.edge_ref) | copy-start | bytes 786436
  25.3 33.5 %collective-permute-start.2 = (s32[72,4096]{1,0:T(8,128)}, s32[72,4096]{1,0:T(8,128)}, u32[]{:S(2)}, u32[]{:S(2)}) collective-permute-start(s32[72,4096]{1,0:T(8,128)} %remap.8.past_ref), channel_id=1, source_target_pairs={{0,1},{1,0},{2,3},{3,2},{4,5},{5,4},{6,7},{7,6},{8,9},{9,8},{10,11... | collective-permute-start | bytes 3538952 | tf_op jit(solution)/shard_map/ppermute | solution.py:860
  44.3 54.2 %collective-permute-start.3 = (s32[72,4096]{1,0:T(8,128)}, s32[72,4096]{1,0:T(8,128)}, u32[]{:S(2)}, u32[]{:S(2)}) collective-permute-start(s32[72,4096]{1,0:T(8,128)} %remap.9.past_ref), channel_id=1, source_target_pairs={{0,1},{1,0},{2,3},{3,2},{4,5},{5,4},{6,7},{7,6},{8,9},{9,8},{10,11... | collective-permute-start | bytes 3538952 | tf_op jit(solution)/shard_map/ppermute | solution.py:860
  44.4 14.5 %copy-start.31 = (f32[2,64,128]{2,1,0:T(8,128)S(1)}, f32[2,64,128]{2,1,0:T(8,128)}, u32[]{:S(2)}) copy-start(f32[2,64,128]{2,1,0:T(8,128)} %constant.117.clone.twiddle_ref) | copy-start | bytes 196612
  44.4 14.5 %copy-start.36 = (bf16[512,512]{1,0:T(8,128)(2,1)S(1)}, bf16[512,512]{1,0:T(8,128)(2,1)}, u32[]{:S(2)}) copy-start(bf16[512,512]{1,0:T(8,128)(2,1)} %constant.114.clone.s_low) | copy-start | bytes 1572868
  44.4 14.5 %copy-start.40 = (bf16[512,512]{1,0:T(8,128)(2,1)S(1)}, bf16[512,512]{1,0:T(8,128)(2,1)}, u32[]{:S(2)}) copy-start(bf16[512,512]{1,0:T(8,128)(2,1)} %constant.113.clone.s_high) | copy-start | bytes 1572868
  44.4 14.5 %copy-start.44 = (bf16[256,256]{1,0:T(8,128)(2,1)S(1)}, bf16[256,256]{1,0:T(8,128)(2,1)}, u32[]{:S(2)}) copy-start(bf16[256,256]{1,0:T(8,128)(2,1)} %constant.106.clone.a_low.refs_7_) | copy-start | bytes 393220
  44.4 14.5 %copy-start.48 = (bf16[256,256]{1,0:T(8,128)(2,1)S(1)}, bf16[256,256]{1,0:T(8,128)(2,1)}, u32[]{:S(2)}) copy-start(bf16[256,256]{1,0:T(8,128)(2,1)} %constant.105.clone.a_high.refs_6_) | copy-start | bytes 393220
  44.4 14.5 %copy-start.54 = (bf16[256,256]{1,0:T(8,128)(2,1)S(1)}, bf16[256,256]{1,0:T(8,128)(2,1)}, u32[]{:S(2)}) copy-start(bf16[256,256]{1,0:T(8,128)(2,1)} %constant.108.clone.b_low) | copy-start | bytes 393220
  44.4 14.5 %copy-start.58 = (bf16[256,256]{1,0:T(8,128)(2,1)S(1)}, bf16[256,256]{1,0:T(8,128)(2,1)}, u32[]{:S(2)}) copy-start(bf16[256,256]{1,0:T(8,128)(2,1)} %constant.107.clone.b_high) | copy-start | bytes 393220
  68.7 58.9 %all-to-all-start = ((s32[32,136,128]{2,1,0:T(8,128)}), s32[32,136,128]{2,1,0:T(8,128)S(1)}, u32[]{:S(2)}, u32[]{:S(2)}) async-start(s32[32,136,128]{2,1,0:T(8,128)} %cols_forward.4.past_ref), calls=%async_computation | async-start | bytes 4456448 | tf_op jit(solution)/shard_map/all_to_all | solution.py:872
  96.6 16.1 %copy-start.32 = (f32[2,64,128]{2,1,0:T(8,128)S(1)}, f32[2,64,128]{2,1,0:T(8,128)}, u32[]{:S(2)}) copy-start(f32[2,64,128]{2,1,0:T(8,128)} %constant.117.clone.twiddle_ref) | copy-start | bytes 196612
  96.6 16.1 %copy-start.37 = (bf16[512,512]{1,0:T(8,128)(2,1)S(1)}, bf16[512,512]{1,0:T(8,128)(2,1)}, u32[]{:S(2)}) copy-start(bf16[512,512]{1,0:T(8,128)(2,1)} %constant.114.clone.s_low) | copy-start | bytes 1572868
  96.6 16.2 %copy-start.41 = (bf16[512,512]{1,0:T(8,128)(2,1)S(1)}, bf16[512,512]{1,0:T(8,128)(2,1)}, u32[]{:S(2)}) copy-start(bf16[512,512]{1,0:T(8,128)(2,1)} %constant.113.clone.s_high) | copy-start | bytes 1572868
  96.6 16.2 %copy-start.45 = (bf16[256,256]{1,0:T(8,128)(2,1)S(1)}, bf16[256,256]{1,0:T(8,128)(2,1)}, u32[]{:S(2)}) copy-start(bf16[256,256]{1,0:T(8,128)(2,1)} %constant.106.clone.a_low.refs_7_) | copy-start | bytes 393220
  96.6 16.2 %copy-start.49 = (bf16[256,256]{1,0:T(8,128)(2,1)S(1)}, bf16[256,256]{1,0:T(8,128)(2,1)}, u32[]{:S(2)}) copy-start(bf16[256,256]{1,0:T(8,128)(2,1)} %constant.105.clone.a_high.refs_6_) | copy-start | bytes 393220
  96.7 16.2 %copy-start.55 = (bf16[256,256]{1,0:T(8,128)(2,1)S(1)}, bf16[256,256]{1,0:T(8,128)(2,1)}, u32[]{:S(2)}) copy-start(bf16[256,256]{1,0:T(8,128)(2,1)} %constant.108.clone.b_low) | copy-start | bytes 393220
  96.7 16.2 %copy-start.59 = (bf16[256,256]{1,0:T(8,128)(2,1)S(1)}, bf16[256,256]{1,0:T(8,128)(2,1)}, u32[]{:S(2)}) copy-start(bf16[256,256]{1,0:T(8,128)(2,1)} %constant.107.clone.b_high) | copy-start | bytes 393220
  96.7 58.8 %collective-permute-start.4 = (s32[72,4096]{1,0:T(8,128)}, s32[72,4096]{1,0:T(8,128)}, u32[]{:S(2)}, u32[]{:S(2)}) collective-permute-start(s32[72,4096]{1,0:T(8,128)} %remap.12), channel_id=1, source_target_pairs={{0,1},{1,0},{2,3},{3,2},{4,5},{5,4},{6,7},{7,6},{8,9},{9,8},{10,11... | collective-permute-start | bytes 3538952 | tf_op jit(solution)/shard_map/ppermute | solution.py:860
  128.9 55.6 %all-to-all-start.1 = ((s32[32,136,128]{2,1,0:T(8,128)}), s32[32,136,128]{2,1,0:T(8,128)S(1)}, u32[]{:S(2)}, u32[]{:S(2)}) async-start(s32[32,136,128]{2,1,0:T(8,128)} %cols_forward.5.past_ref), calls=%async_computation.1 | async-start | bytes 4456448 | tf_op jit(solution)/shard_map/all_to_all | solution.py:872
  137.4 18.1 %copy-start.22 = (bf16[128,768]{1,0:T(8,128)(2,1)S(1)}, bf16[128,768]{1,0:T(8,128)(2,1)}, u32[]{:S(2)}) copy-start(bf16[128,768]{1,0:T(8,128)(2,1)} %constant.120.clone.moves_ref) | copy-start | bytes 589828
  153.6 17.1 %copy-start.3 = (s32[32,136,128]{2,1,0:T(8,128)S(1)}, s32[32,136,128]{2,1,0:T(8,128)}, u32[]{:S(2)}) copy-start(s32[32,136,128]{2,1,0:T(8,128)} %copy-done.2) | copy-start | bytes 6684676
  153.6 17.1 %copy-start.15 = (f32[2,128,64]{2,1,0:T(8,128)S(1)}, f32[2,128,64]{2,1,0:T(8,128)}, u32[]{:S(2)}) copy-start(f32[2,128,64]{2,1,0:T(8,128)} %constant.118.clone.twiddle_ref) | copy-start | bytes 196612
  153.6 37.3 %collective-permute-start.5 = (s32[72,4096]{1,0:T(8,128)}, s32[72,4096]{1,0:T(8,128)}, u32[]{:S(2)}, u32[]{:S(2)}) collective-permute-start(s32[72,4096]{1,0:T(8,128)} %remap.14), channel_id=1, source_target_pairs={{0,1},{1,0},{2,3},{3,2},{4,5},{5,4},{6,7},{7,6},{8,9},{9,8},{10,11... | collective-permute-start | bytes 3538952 | tf_op jit(solution)/shard_map/ppermute | solution.py:860
  185.9 56.5 %all-to-all-start.2 = ((s32[32,136,128]{2,1,0:T(8,128)}), s32[32,136,128]{2,1,0:T(8,128)S(1)}, u32[]{:S(2)}, u32[]{:S(2)}) async-start(s32[32,136,128]{2,1,0:T(8,128)} %cols_forward.6), calls=%async_computation.2 | async-start | bytes 4456448 | tf_op jit(solution)/shard_map/all_to_all | solution.py:872
  190.9 18.4 %copy-start.1 = (s32[32,136,128]{2,1,0:T(8,128)S(1)}, s32[32,136,128]{2,1,0:T(8,128)}, u32[]{:S(2)}) copy-start(s32[32,136,128]{2,1,0:T(8,128)} %copy-done) | copy-start | bytes 6684676
  223.3 22.9 %copy-start.63 = (s32[128]{0:T(128)S(1)}, s32[128]{0:T(128)}, u32[]{:S(2)}) copy-start(s32[128]{0:T(128)} %constant.134) | copy-start | bytes 1540
  223.3 22.9 %copy-start.64 = (s32[128]{0:T(128)S(1)}, s32[128]{0:T(128)}, u32[]{:S(2)}) copy-start(s32[128]{0:T(128)} %constant.119.clone) | copy-start | bytes 1540
  242.4 55.3 %all-to-all-start.3 = ((s32[32,136,128]{2,1,0:T(8,128)}), s32[32,136,128]{2,1,0:T(8,128)}, u32[]{:S(2)}, u32[]{:S(2)}) async-start(s32[32,136,128]{2,1,0:T(8,128)} %cols_forward.7), calls=%async_computation.3 | async-start | bytes 4456448 | tf_op jit(solution)/shard_map/all_to_all | solution.py:872
  250.9 53.0 %copy-start.52 = (bf16[256,256]{1,0:T(8,128)(2,1)S(1)}, bf16[256,256]{1,0:T(8,128)(2,1)}, u32[]{:S(2)}) copy-start(bf16[256,256]{1,0:T(8,128)(2,1)} %constant.110.clone.refs_5_) | copy-start | bytes 393220
  250.9 53.0 %copy-start.53 = (bf16[256,256]{1,0:T(8,128)(2,1)S(1)}, bf16[256,256]{1,0:T(8,128)(2,1)}, u32[]{:S(2)}) copy-start(bf16[256,256]{1,0:T(8,128)(2,1)} %constant.109.clone.refs_4_) | copy-start | bytes 393220
  335.6 32.7 %all-to-all-start.5 = ((s32[32,72,128]{2,1,0:T(8,128)}), s32[32,72,128]{2,1,0:T(8,128)S(1)}, u32[]{:S(2)}, u32[]{:S(2)}) async-start(s32[32,72,128]{2,1,0:T(8,128)} %rows_inverse.5), calls=%async_computation.5 | async-start | bytes 2359296 | tf_op jit(solution)/shard_map/all_to_all | solution.py:881
  345.5 26.7 %copy-start.27 = (bf16[256,256]{1,0:T(8,128)(2,1)S(1)}, bf16[256,256]{1,0:T(8,128)(2,1)}, u32[]{:S(2)}) copy-start(bf16[256,256]{1,0:T(8,128)(2,1)} %constant.116.clone.s_low) | copy-start | bytes 393220
  345.5 26.7 %copy-start.28 = (bf16[256,256]{1,0:T(8,128)(2,1)S(1)}, bf16[256,256]{1,0:T(8,128)(2,1)}, u32[]{:S(2)}) copy-start(bf16[256,256]{1,0:T(8,128)(2,1)} %constant.115.clone.s_high) | copy-start | bytes 393220
  345.5 26.7 %copy-start.29 = (bf16[256,256]{1,0:T(8,128)(2,1)S(1)}, bf16[256,256]{1,0:T(8,128)(2,1)}, u32[]{:S(2)}) copy-start(bf16[256,256]{1,0:T(8,128)(2,1)} %constant.112.clone.g_low) | copy-start | bytes 393220
  345.5 26.7 %copy-start.30 = (bf16[256,256]{1,0:T(8,128)(2,1)S(1)}, bf16[256,256]{1,0:T(8,128)(2,1)}, u32[]{:S(2)}) copy-start(bf16[256,256]{1,0:T(8,128)(2,1)} %constant.111.clone.g_high) | copy-start | bytes 393220
  368.3 32.9 %all-to-all-start.4 = ((s32[32,72,128]{2,1,0:T(8,128)}), s32[32,72,128]{2,1,0:T(8,128)S(1)}, u32[]{:S(2)}, u32[]{:S(2)}) async-start(s32[32,72,128]{2,1,0:T(8,128)} %copy-done.24), calls=%async_computation.4 | async-start | bytes 2359296 | tf_op jit(solution)/shard_map/all_to_all | solution.py:881
  401.2 32.7 %all-to-all-start.7 = ((s32[32,72,128]{2,1,0:T(8,128)}), s32[32,72,128]{2,1,0:T(8,128)S(1)}, u32[]{:S(2)}, u32[]{:S(2)}) async-start(s32[32,72,128]{2,1,0:T(8,128)} %copy-done.26), calls=%async_computation.7 | async-start | bytes 2359296 | tf_op jit(solution)/shard_map/all_to_all | solution.py:881
  433.9 46.0 %all-to-all-start.6 = ((s32[32,72,128]{2,1,0:T(8,128)}), s32[32,72,128]{2,1,0:T(8,128)S(1)}, u32[]{:S(2)}, u32[]{:S(2)}) async-start(s32[32,72,128]{2,1,0:T(8,128)} %copy-done.25), calls=%async_computation.6 | async-start | bytes 2359296 | tf_op jit(solution)/shard_map/all_to_all | solution.py:881
  437.5 28.2 %collective-permute-start.7 = (s32[72,2048]{1,0:T(8,128)}, s32[72,2048]{1,0:T(8,128)S(1)}, u32[]{:S(2)}, u32[]{:S(2)}) collective-permute-start(s32[72,2048]{1,0:T(8,128)} %copy-done.35), channel_id=1, source_target_pairs={{0,1},{1,0},{2,3},{3,2},{4,5},{5,4},{6,7},{7,6},{8,9},{9,8},{10,11... | collective-permute-start | bytes 1769480 | tf_op jit(solution)/shard_map/ppermute | solution.py:888
  439.3 39.4 %collective-permute-start.6 = (s32[72,2048]{1,0:T(8,128)}, s32[72,2048]{1,0:T(8,128)S(1)}, u32[]{:S(2)}, u32[]{:S(2)}) collective-permute-start(s32[72,2048]{1,0:T(8,128)} %copy-done.34), channel_id=1, source_target_pairs={{0,1},{1,0},{2,3},{3,2},{4,5},{5,4},{6,7},{7,6},{8,9},{9,8},{10,11... | collective-permute-start | bytes 1769480 | tf_op jit(solution)/shard_map/ppermute | solution.py:888
  471.3 20.1 %collective-permute-start.9 = (s32[72,2048]{1,0:T(8,128)}, s32[72,2048]{1,0:T(8,128)S(1)}, u32[]{:S(2)}, u32[]{:S(2)}) collective-permute-start(s32[72,2048]{1,0:T(8,128)} %get-tuple-element.31), channel_id=1, source_target_pairs={{0,1},{1,0},{2,3},{3,2},{4,5},{5,4},{6,7},{7,6},{8,9},{9,8},{10,11... | collective-permute-start | bytes 1769480 | tf_op jit(solution)/shard_map/ppermute | solution.py:888
  484.1 19.5 %collective-permute-start.8 = (s32[72,2048]{1,0:T(8,128)S(1)}, s32[72,2048]{1,0:T(8,128)S(1)}, u32[]{:S(2)}, u32[]{:S(2)}) collective-permute-start(s32[72,2048]{1,0:T(8,128)S(1)} %get-tuple-element.30), channel_id=1, source_target_pairs={{0,1},{1,0},{2,3},{3,2},{4,5},{5,4},{6,7},{7,6},{8,9},{9,8},{10,11... | collective-permute-start | bytes 1769480 | tf_op jit(solution)/shard_map/ppermute | solution.py:888
  (35 other events, 96.3 us)
